TPU v7x, 1024 devices: a whole 8x8x8 slice. The times are simulated.
1024 devices in a mesh: grp: 64 (over z, y), loc: 16 (over x, core).
Axes of the slice: x: 8, y: 8, z: 8, core: 2. Of those that a mesh axis runs over, the one named last changes fastest.
Arguments:
- out_grad: bfloat16 [8192, 7168], P(('grp', 'loc')), may hold values from -6 to 6
- route_prob: bfloat16 [8192, 4, 2], P(('grp', 'loc')), may hold values from 0.019897461 to 1
- group_ids: int32 [8192, 4], P(('grp', 'loc')), may hold values from 0 to 63, as said below
- gate_pre: bfloat16 [64, 512, 2048], P('grp', None, 'loc'), may hold values from -6 to 6
- down_weight: bfloat16 [131072, 7168], P(('grp', 'loc')), may hold values from -0.0625 to 0.0625
Outputs:
- pre_grad: bfloat16 [64, 512, 2048], P('grp', None, 'loc')
- route_grad: float32 [8192, 4, 2], P(('grp', 'loc'))
Inputs may be any that keep to these rules, and one draw needn't show every extreme that they name: `group_ids`: for device (g, l) and its row s = t * 4 + k, the group is (g + p_l(s mod 64)) mod 64, with one permutation p_l of the groups for each index l of loc; so a token's 4 groups differ, every row of every group is filled exactly once, and a device names one group at most 1 times.
All inputs are finite; a program needn't handle non-finite values.
Results may differ from a plain program's by a relative error of at most 0.0012.
Values may be sent and summed in bfloat16 or wider, within the bound.
No kernel may reach another device: no remote copies, remote signals or barrier semaphores. Data moves between devices by JAX's collectives and lax.ppermute only.
A program may use at most 32 MiB of HBM per device.

v0:
```python
import jax
import jax.numpy as jnp
from jax import lax
from jax.sharding import PartitionSpec as P


def local_terms(grad_rows, prob_rows, gate_rows, down_weight, expert_pick):
    hidden_grad = lax.dot_general(
        grad_rows, down_weight, (((1,), (1,)), ((), ())), preferred_element_type=jnp.float32
    )
    gate_value = gate_rows.astype(jnp.float32)
    sigma = jax.nn.sigmoid(gate_value)
    active = gate_value * sigma
    slope = sigma * (1.0 + gate_value * (1.0 - sigma))
    scale = jnp.sum(prob_rows.astype(jnp.float32) * expert_pick, axis=1)
    grad_out = (scale[:, None] * hidden_grad * slope).astype(jnp.bfloat16)
    prob_grad = jnp.sum(active * hidden_grad, axis=1)[:, None] * expert_pick
    return (grad_out, prob_grad)


def body(out_grad, route_prob, group_ids, gate_pre, down_weight):
    tok_dev = out_grad.shape[0]
    top_count = group_ids.shape[1]
    expert_count = route_prob.shape[2]
    grp_count = lax.axis_size("grp")
    loc_count = lax.axis_size("loc")
    split_size = loc_count // expert_count
    rows_lane = tok_dev * top_count
    capacity = (rows_lane + grp_count - 1) // grp_count
    my_group = lax.axis_index("grp")
    my_expert = lax.axis_index("loc") // split_size
    expert_pick = (jnp.arange(expert_count, dtype=jnp.int32) == my_expert).astype(jnp.float32)
    row_ids = jnp.arange(rows_lane, dtype=jnp.int32)
    dest_grp = group_ids.reshape(rows_lane)
    slot_index = row_ids // grp_count
    send_pos = dest_grp * capacity + slot_index
    source_pos = (2 * my_group - dest_grp) % grp_count * capacity + slot_index
    buffer_ids = jnp.arange(grp_count * capacity, dtype=jnp.int32)
    send_table = buffer_ids[:, None] == send_pos[None, :]
    recv_table = source_pos[:, None] == buffer_ids[None, :]
    grad_rows = jnp.repeat(out_grad, top_count, axis=0)
    prob_rows = route_prob.reshape(rows_lane, expert_count)
    send_bf = send_table.astype(jnp.bfloat16)
    send_grad = jnp.dot(send_bf, grad_rows, preferred_element_type=jnp.float32).astype(jnp.bfloat16)
    send_prob = jnp.dot(send_bf, prob_rows, preferred_element_type=jnp.float32).astype(jnp.bfloat16)
    send_grad = send_grad.reshape(grp_count, capacity, grad_rows.shape[1])
    send_prob = send_prob.reshape(grp_count, capacity, expert_count)
    recv_grad, recv_prob = (
        lax.all_to_all(send_grad, "grp", split_axis=0, concat_axis=0, tiled=True),
        lax.all_to_all(send_prob, "grp", split_axis=0, concat_axis=0, tiled=True),
    )
    recv_bf = recv_table.astype(jnp.bfloat16)
    lane_grad = jnp.dot(
        recv_bf, recv_grad.reshape(grp_count * capacity, -1), preferred_element_type=jnp.float32
    ).astype(jnp.bfloat16)
    lane_prob = jnp.dot(
        recv_bf,
        recv_prob.reshape(grp_count * capacity, expert_count),
        preferred_element_type=jnp.float32,
    ).astype(jnp.bfloat16)
    gate_rows = gate_pre[0]
    group_grad, group_prob = (
        lax.all_gather(lane_grad, "loc", axis=0, tiled=True),
        lax.all_gather(lane_prob, "loc", axis=0, tiled=True),
    )
    grad_out, prob_grad = local_terms(group_grad, group_prob, gate_rows, down_weight, expert_pick)
    lane_sums = lax.psum_scatter(prob_grad, "loc", scatter_dimension=0, tiled=True)
    back_send = jnp.dot(
        recv_table.T.astype(jnp.float32), lane_sums, precision=lax.Precision.HIGHEST
    )
    back_send = back_send.reshape(grp_count, capacity, expert_count)
    back_recv = lax.all_to_all(back_send, "grp", split_axis=0, concat_axis=0, tiled=True)
    route_grad = jnp.dot(
        send_table.T.astype(jnp.float32),
        back_recv.reshape(grp_count * capacity, expert_count),
        precision=lax.Precision.HIGHEST,
    )
    return (grad_out[None], route_grad.reshape(tok_dev, top_count, expert_count))


def solution(mesh):
    placed = (
        P(("grp", "loc"), None),
        P(("grp", "loc"), None, None),
        P(("grp", "loc"), None),
        P("grp", None, "loc"),
        P(("grp", "loc"), None),
    )
    return jax.shard_map(
        body,
        mesh=mesh,
        in_specs=placed,
        out_specs=(P("grp", None, "loc"), P(("grp", "loc"), None, None)),
        check_vma=False,
    )
```

profile of v0, /device:TPU:1, one launch (start us, length us, event | category | flops | bytes accessed | tf_op | source)
XLA Modules:
  0.0 224.2 jit_solution(43408719421797231)
XLA Ops:
  7.2 0.0 copy-start
  7.2 0.0 all-gather.3.cloned.1.call-start
  7.2 0.9 copy.39
  8.1 0.1 reshape.114
  8.2 1.0 broadcast_in_dim.4
  9.2 0.1 reshape.118
  9.3 0.4 fusion
  9.7 0.5 broadcast.117
  10.2 2.0 reduce
  12.2 2.8 %reshape.130 = bf16[64,2,3584]{2,1,0:T(2,128)(2,1)S(1)} reshape(bf16[64,7168]{1,0:T(8,128)(2,1)} %reduce) | data formatting | bytes 1835008
  15.0 48.9 %all_to_all.15 = bf16[64,2,3584]{2,1,0:T(2,128)(2,1)} all-to-all(bf16[64,2,3584]{2,1,0:T(2,128)(2,1)S(1)} %reshape.130), channel_id=1, replica_groups=mesh['grp'=64,'loc'=16] {'grp'}, dimensions={0} | all-to-all | bytes 1835008 | tf_op jit(solution)/shard_map/all_to_all | solution.py:49
  63.9 0.0 copy-start.2
  63.9 0.0 copy-start.1
  63.9 6.4 %reshape.131 = bf16[64,1,7168]{2,1,0:T(2,128)(2,1)} reshape(bf16[64,2,3584]{2,1,0:T(2,128)(2,1)} %all_to_all.15) | data formatting | bytes 1835008
  70.3 2.7 %convolution_convert_fusion.1 = bf16[32,7168]{1,0:T(8,128)(2,1)} fusion(bf16[64,1,7168]{2,1,0:T(2,128)(2,1)} %reshape.131, s32[32]{0:T(128)S(1)} %get-tuple-element.14), kind=kOutput, calls=%fused_computation.2 | convolution fusion | flops 29591552 | bytes 1376384 | tf_op jit(solution)/shard_map/dot_general | solution.py:53
  73.0 0.0 all-gather.3.cloned.1.call-update
  73.0 0.0 copy-done.2
  73.0 0.1 copy.40
  73.1 0.1 reshape.115
  73.2 0.1 fusion.1
  73.3 0.7 copy.41
  74.1 7.4 %all-to-all-start = ((bf16[64,1,2]{2,1,0:T(2,128)(2,1)}), bf16[64,1,2]{2,1,0:T(2,128)(2,1)S(1)}, u32[]{:S(2)}, u32[]{:S(2)}) async-start(bf16[64,1,2]{2,1,0:T(2,128)(2,1)} %copy.41), calls=%async_computation | async-start | bytes 65536 | tf_op jit(solution)/shard_map/all_to_all | solution.py:50
  81.5 0.0 reduce-scatter.4.cloned.1.call-start
  81.6 0.0 copy-done.1
  81.6 0.1 copy.45
  81.7 10.6 %all-to-all-done = bf16[64,1,2]{2,1,0:T(2,128)(2,1)S(1)} async-done(((bf16[64,1,2]{2,1,0:T(2,128)(2,1)}), bf16[64,1,2]{2,1,0:T(2,128)(2,1)S(1)}, u32[]{:S(2)}, u32[]{:S(2)}) %all-to-all-start) | async-done | bytes 288 | tf_op jit(solution)/shard_map/all_to_all | solution.py:50
  92.3 0.1 copy.42
  92.4 0.2 fusion.2
  92.6 19.6 %all-gather = bf16[16,32,2]{1,2,0:T(2,128)(2,1)S(1)} all-gather(bf16[1,32,2]{1,2,0:T(2,128)(2,1)S(1)} %fusion.2), channel_id=1, replica_groups=mesh['grp'=64,'loc'=16] {'loc'}, dimensions={0}, use_global_device_ids=true | all-gather | bytes 2176 | tf_op jit(solution)/shard_map/all_gather | solution.py:64
  112.2 0.1 reshape.126
  112.3 0.1 multiply_reduce_fusion
  112.4 13.5 %all-gather.3.cloned.1.call-done = bf16[512,7168]{1,0:T(8,128)(2,1)} async-done(((bf16[32,7168]{1,0:T(8,128)(2,1)}), bf16[512,7168]{1,0:T(8,128)(2,1)}) %all-gather.3.cloned.1.call-update) | async-done | bytes 7340048 | tf_op jit(solution)/shard_map/all_gather | solution.py:63
  125.9 0.0 copy-done
  125.9 5.7 %fusion.13 = (f32[512]{0:T(512)S(1)}, bf16[1,512,128]{1,2,0:T(8,128)(2,1)S(1)}) fusion(bf16[1,512,128]{1,2,0:T(8,128)(2,1)S(1)} %copy.45, f32[512]{0:T(512)S(1)} %multiply_reduce_fusion, bf16[512,7168]{1,0:T(8,128)(2,1)} %all-gather.3.cloned.1.call-done, bf16[128,7168]{1,0:T(8,128)(2,1)S(1)} %copy-done), kind=kOutput, calls=%fused_computation.20 | convolution fusion | flops 940441088 | bytes 9441280 | tf_op jit(solution)/shard_map/dot_general | solution.py:8
  131.6 0.1 broadcast_multiply_fusion
  131.6 0.9 copy.50
  132.5 0.0 reduce-scatter.4.cloned.1.call-update
  132.5 60.2 %reduce-scatter.4.cloned.1.call-done = f32[32,2]{1,0:T(8,128)} async-done(((f32[512,2]{1,0:T(8,128)}), f32[32,2]{1,0:T(8,128)}) %reduce-scatter.4.cloned.1.call-update) | async-done | bytes 272
  192.7 1.6 fusion.17
  194.3 11.4 %all-to-all-start.2 = ((f32[64,1,2]{2,1,0:T(1,128)}), f32[64,1,2]{2,1,0:T(1,128)S(1)}, u32[]{:S(2)}, u32[]{:S(2)}) async-start(f32[64,1,2]{2,1,0:T(1,128)} %bitcast.14), calls=%async_computation.2 | async-start | bytes 65536 | tf_op jit(solution)/shard_map/all_to_all | solution.py:72
  205.7 0.1 iota_compare_fusion.3
  205.8 0.8 copy.49
  206.5 10.0 %all-to-all-done.2 = f32[64,1,2]{2,1,0:T(1,128)S(1)} async-done(((f32[64,1,2]{2,1,0:T(1,128)}), f32[64,1,2]{2,1,0:T(1,128)S(1)}, u32[]{:S(2)}, u32[]{:S(2)}) %all-to-all-start.2) | async-done | bytes 544 | tf_op jit(solution)/shard_map/all_to_all | solution.py:72
  216.5 0.9 fusion.18
  (3 shorter events, 0.0 us)
Async XLA Ops:
  7.2 118.7 %copy-start = (bf16[128,7168]{1,0:T(8,128)(2,1)S(1)}, bf16[128,7168]{1,0:T(8,128)(2,1)}, u32[]{:S(2)}) copy-start(bf16[128,7168]{1,0:T(8,128)(2,1)} %param.9) | copy-start | bytes 5505028
  7.2 118.7 %all-gather.3.cloned.1.call-start = ((), (), s32[]{:S(2)}) async-start(), calls=%async_computation.4 | async-start | bytes 7798784 | tf_op jit(solution)/shard_map/all_gather | solution.py:63
  63.9 9.1 %copy-start.2 = (bf16[8,4,2]{0,2,1:T(2,128)(2,1)S(1)}, bf16[8,4,2]{0,2,1:T(2,128)(2,1)}, u32[]{:S(2)}) copy-start(bf16[8,4,2]{0,2,1:T(2,128)(2,1)} %param.6) | copy-start | bytes 388
  63.9 17.7 %copy-start.1 = (bf16[1,512,128]{2,1,0:T(8,128)(2,1)S(1)}, bf16[1,512,128]{2,1,0:T(8,128)(2,1)}, u32[]{:S(2)}) copy-start(bf16[1,512,128]{2,1,0:T(8,128)(2,1)} %param.8) | copy-start | bytes 393220
  74.1 18.2 %all-to-all-start = ((bf16[64,1,2]{2,1,0:T(2,128)(2,1)}), bf16[64,1,2]{2,1,0:T(2,128)(2,1)S(1)}, u32[]{:S(2)}, u32[]{:S(2)}) async-start(bf16[64,1,2]{2,1,0:T(2,128)(2,1)} %copy.41), calls=%async_computation | async-start | bytes 65536 | tf_op jit(solution)/shard_map/all_to_all | solution.py:50
  81.5 111.2 %reduce-scatter.4.cloned.1.call-start = ((), (), s32[]{:S(2)}) async-start(), calls=%async_computation.5 | async-start | bytes 278528
  194.3 22.2 %all-to-all-start.2 = ((f32[64,1,2]{2,1,0:T(1,128)}), f32[64,1,2]{2,1,0:T(1,128)S(1)}, u32[]{:S(2)}, u32[]{:S(2)}) async-start(f32[64,1,2]{2,1,0:T(1,128)} %bitcast.14), calls=%async_computation.2 | async-start | bytes 65536 | tf_op jit(solution)/shard_map/all_to_all | solution.py:72
Sparse Core Ops, SparseCore 0:
  73.1 52.7 all-gather.2
  132.6 60.0 reduce-scatter.3
where the time goes:
time: 227 us; the launch traced here: 224 us
  waiting for transfers between devices  94.3 us (42%)
  blocking collectives  68.5 us (30%)
  starting transfers between devices  18.9 us (8%)
  local copies, waits for them, and re-layouts  14.7 us (6%)
  between operations  14.2 us (6%)
  matrix products  11.5 us (5%)
    unnamed x3, waiting for transfers between devices  60.2 us
    all_to_all x1, blocking collectives, body(): lax.all_to_all(send_grad, 'grp', split_axis=0, concat_axis=0, tiled=True)  48.9 us
    all_gather x1, blocking collectives, body(): lax.all_gather(lane_prob, 'loc', axis=0, tiled=True)  19.6 us
    all_gather x1, waiting for transfers between devices, body(): lax.all_gather(lane_grad, 'loc', axis=0, tiled=True)  13.5 us
    unnamed x13, local copies, waits for them, and re-layouts  11.9 us
    all_to_all x1, starting transfers between devices, body(): lax.all_to_all(back_send, 'grp', split_axis=0, concat_axis=0, tiled=True)  11.4 us
    all_to_all x1, waiting for transfers between devices, body(): lax.all_to_all(send_prob, 'grp', split_axis=0, concat_axis=0, tiled=True)  10.6 us
    all_to_all x1, waiting for transfers between devices, body(): lax.all_to_all(back_send, 'grp', split_axis=0, concat_axis=0, tiled=True)  9.99 us
  transfers between devices with their start and end apart: 4, of which 4 were waited for; matrix products, arithmetic and copies ran while one was open for 1% of the time, Pallas kernels for 0%

commit v1 on v0

v1 whole, which is shorter than its diff:
```python
import functools

import jax
import jax.numpy as jnp
from jax import lax
from jax.experimental import pallas as pl
from jax.experimental.pallas import tpu as pltpu
from jax.sharding import PartitionSpec as P

SUB = 8
LANES = 128
SHARES = (7,)
NT = (((1,), (1,)), ((), ()))
TN = (((0,), (0,)), ((), ()))
BF = jnp.bfloat16
F32 = jnp.float32


def iota(shape, dim):
    return lax.broadcasted_iota(jnp.int32, shape, dim)


def chunks(model):
    unit, found, first = model // sum(SHARES), [], 0
    for share in SHARES:
        found.append((first, unit * share // SUB))
        first += unit * share
    return found


def send_kernel(grad_ref, gid_ref, prob_ref, *out_refs):
    tok = grad_ref.shape[0]
    rows = out_refs[0].shape[0]
    shape = (rows, SUB * tok)
    row, col = iota(shape, 0), iota(shape, 1)
    same_sub = (row % SUB) == (col // tok)
    slot = row // SUB
    pick = jnp.zeros(shape, F32)
    prob = jnp.zeros((rows, prob_ref.shape[1]), F32)
    for k in range(gid_ref.shape[0]):
        here = jnp.where(same_sub & (slot == gid_ref[k : k + 1, :]), 1.0, 0.0)
        pick += here
        prob += lax.dot_general(here.astype(BF), prob_ref[k], NT, preferred_element_type=F32)
    for out_ref, (first, wide) in zip(out_refs, chunks(grad_ref.shape[1])):
        starts = [first + e * wide for e in range(SUB)]
        grad = jnp.concatenate([grad_ref[:, at : at + wide] for at in starts], axis=0)
        out_ref[:, :wide] = jnp.dot(pick.astype(BF), grad, preferred_element_type=F32).astype(BF)
    out_refs[-1][:, wide:] = prob.astype(BF)


def pick_kernel(recv_ref, source_ref, *refs):
    out_ref = refs[-1]
    rows = source_ref.shape[0]
    wide = out_ref.shape[1]
    lane_rows = rows // SUB
    pick = jnp.where(iota((rows, recv_ref.shape[0]), 1) == source_ref[...], 1.0, 0.0).astype(BF)
    out_ref[:rows, :] = jnp.dot(pick, recv_ref[:, :wide], preferred_element_type=F32).astype(BF)
    if out_ref.shape[0] == rows:
        return
    prob = jnp.dot(pick[:lane_rows], recv_ref[:, wide:], preferred_element_type=F32)
    prob = jnp.transpose(prob)[:SUB]
    pad = jnp.zeros((SUB, wide - lane_rows), F32)
    out_ref[rows:, :] = jnp.concatenate([prob, pad], axis=1).astype(BF)


def terms_kernel(place_ref, *refs):
    parts, (own_w, mate_w, own_gate, mate_gate, pre_ref, give_ref, sum_ref) = refs[:-7], refs[-7:]
    count = len(parts) // len(SHARES)
    shards = parts[-count:]
    rows = (shards[0].shape[0] - SUB) // SUB
    width = own_w.shape[0]
    hidden = jnp.zeros((count * rows, 2 * width), F32)
    for c, (first, wide) in enumerate(chunks(own_w.shape[1])):
        here = parts[c * count : (c + 1) * count]
        for e in range(SUB):
            left = jnp.concatenate([ref[e * rows : (e + 1) * rows, :] for ref in here], axis=0)
            cols = slice(first + e * wide, first + (e + 1) * wide)
            right = jnp.concatenate([own_w[:, cols], mate_w[:, cols]], axis=0)
            hidden += lax.dot_general(left, right, NT, preferred_element_type=F32)
    expert = jnp.where(iota((SUB, width), 0) == place_ref[count], 1.0, 0.0).astype(BF)
    terms = []
    for i, ref in enumerate(shards):
        at = pl.ds(pl.multiple_of(place_ref[i] * rows, rows), rows)
        scale = lax.dot_general(
            ref[SUB * rows :, :rows], expert, TN, preferred_element_type=F32
        )
        total = jnp.zeros((rows, width), F32)
        for half, gate in enumerate((own_gate, mate_gate)):
            grad = hidden[i * rows : (i + 1) * rows, half * width : (half + 1) * width]
            value = gate[at, :].astype(F32)
            sigma = jax.nn.sigmoid(value)
            slope = sigma * (1.0 + value * (1.0 - sigma))
            total += value * sigma * grad
            result = (scale * grad * slope).astype(BF)
            if half == 0:
                pre_ref[at, :] = result
            else:
                give_ref[i * rows : (i + 1) * rows, :] = result
        terms.append(total)
    sums = lax.dot_general(
        jnp.ones((SUB, width), F32),
        jnp.concatenate(terms, axis=0),
        NT,
        precision=lax.Precision.HIGHEST,
        preferred_element_type=F32,
    )
    sum_ref[...] = jnp.zeros(sum_ref.shape, F32)
    for i in range(count):
        sum_ref[pl.ds(place_ref[i], 1), 0, :rows] = sums[:1, i * rows : (i + 1) * rows]


def join_kernel(place_ref, half_ref, got_ref, out_ref):
    rows = got_ref.shape[0] // place_ref.shape[0]
    out_ref[...] = half_ref[...]
    for i in range(place_ref.shape[0]):
        at = pl.ds(pl.multiple_of(place_ref[i] * rows, rows), rows)
        out_ref[at, :] = got_ref[i * rows : (i + 1) * rows, :]


VMEM = pl.BlockSpec(memory_space=pltpu.VMEM)
SMEM = pl.BlockSpec(memory_space=pltpu.SMEM)
ANY = pl.BlockSpec(memory_space=pl.ANY)
PARAMS = pltpu.CompilerParams(vmem_limit_bytes=48 * 1024 * 1024)


def call(kernel, specs, shapes, *args):
    single = not isinstance(shapes, list)
    return pl.pallas_call(
        kernel,
        in_specs=specs,
        out_specs=VMEM if single else [VMEM] * len(shapes),
        out_shape=shapes,
        compiler_params=PARAMS,
    )(*args)


def shape(dims, kind):
    return jax.ShapeDtypeStruct(dims, kind)


def body(out_grad, route_prob, group_ids, gate_pre, down_weight):
    tok, model = out_grad.shape
    top = group_ids.shape[1]
    experts = route_prob.shape[2]
    groups = lax.axis_size("grp")
    locs = lax.axis_size("loc")
    chips = locs // 2
    rows = tok * top
    gate_rows = gate_pre[0]
    width = gate_rows.shape[1]
    my_group = lax.axis_index("grp")
    loc = lax.axis_index("loc")
    swap = [(l, l ^ 1) for l in range(locs)]
    ahead = [(l, (l + (2 if l % 2 == 0 else -2)) % locs) for l in range(locs)]

    gid = jnp.tile(group_ids.T, (1, SUB))
    prob = jnp.pad(
        jnp.transpose(route_prob, (1, 2, 0)), ((0, 0), (0, LANES - experts), (0, 0))
    )
    prob = jnp.tile(prob, (1, 1, SUB))
    plan = chunks(model)
    extra = [LANES if c == len(plan) - 1 else 0 for c in range(len(plan))]
    sends = call(
        send_kernel,
        [VMEM] * 3,
        [shape((groups * SUB, wide + more), BF) for (_, wide), more in zip(plan, extra)],
        out_grad,
        gid,
        prob,
    )
    move = functools.partial(lax.ppermute, axis_name="loc")
    recvs = [
        lax.all_to_all(
            send.reshape(groups, SUB, -1), "grp", split_axis=0, concat_axis=0, tiled=True
        ).reshape(groups * SUB, -1)
        for send in sends
    ]
    mate_w = move(down_weight, perm=swap)
    mate_gate = move(gate_rows, perm=swap)
    flat = group_ids.reshape(rows)
    source = (2 * my_group - flat) % groups
    source = (source[None, :] * SUB + jnp.arange(SUB, dtype=jnp.int32)[:, None]).reshape(-1, 1)
    nears, fars = [], []
    for c, (_, wide) in enumerate(plan):
        early = (mate_w, mate_gate) if c == 0 else ()
        own = call(
            pick_kernel,
            [VMEM] * 2 + [ANY] * len(early),
            shape((SUB * rows + (SUB if extra[c] else 0), wide), BF),
            recvs[c],
            source,
            *early,
        )
        nears.append([own])
        fars.append([move(own, perm=swap)])
    for step in range(chips // 2):
        for near, far in zip(nears, fars):
            near.append(move(near[-1], perm=ahead))
            if step < chips // 2 - 1:
                far.append(move(far[-1], perm=ahead))
    shards = [one for near, far in zip(nears, fars) for one in near + far[1:]]
    count = len(shards) // len(plan)

    def places(at):
        chip, core = at // 2, at % 2
        step = 2 * core - 1
        hops = [(k, core) for k in range(chips // 2 + 1)] + [(k, 1 - core) for k in range(1, chips // 2)]
        return jnp.stack([(chip + step * k) % chips * 2 + c for k, c in hops]).astype(jnp.int32)

    place = jnp.concatenate([places(loc), (loc // (locs // experts)).reshape(1)])
    half, give, sums = call(
        terms_kernel,
        [SMEM] + [VMEM] * (len(shards) + 4),
        [
            shape(gate_rows.shape, BF),
            shape((count * rows, width), BF),
            shape((locs, 1, LANES), F32),
        ],
        place,
        *shards,
        down_weight,
        mate_w,
        gate_rows,
        mate_gate,
    )
    got = move(give, perm=swap)
    parts = lax.all_to_all(sums, "loc", split_axis=0, concat_axis=0, tiled=True)
    lane = jnp.sum(parts.reshape(experts, locs // experts, LANES), axis=1)
    lane = jnp.pad(lane[:, :rows].reshape(experts * rows), (0, LANES - experts * rows))
    back = lax.all_to_all(
        jnp.broadcast_to(lane, (groups, 1, LANES)), "grp", split_axis=0, concat_axis=0, tiled=True
    )[:, 0]
    pre = call(join_kernel, [SMEM, VMEM, VMEM], shape(gate_rows.shape, BF), places(loc ^ 1), half, got)
    wanted = jnp.tile(flat, experts)[None, :] == jnp.arange(groups, dtype=jnp.int32)[:, None]
    route = jnp.sum(jnp.where(wanted, back[:, : experts * rows], 0.0), axis=0)
    route = jnp.transpose(route.reshape(experts, tok, top), (1, 2, 0))
    return pre[None], route


def solution(mesh):
    placed = (
        P(("grp", "loc"), None),
        P(("grp", "loc"), None, None),
        P(("grp", "loc"), None),
        P("grp", None, "loc"),
        P(("grp", "loc"), None),
    )
    return jax.shard_map(
        body,
        mesh=mesh,
        in_specs=placed,
        out_specs=(P("grp", None, "loc"), P(("grp", "loc"), None, None)),
        check_vma=False,
    )
```

time: 227 us -> 151 us (0.67)
  blocking collectives: 68.5 us -> 0 us
  starting transfers between devices: 18.9 us -> 86.1 us
  waiting for transfers between devices: 94.3 us -> 44.9 us
  between operations: 14.2 us -> 1.08 us
  matrix products: 11.5 us -> 0 us
  Pallas kernels: 0 us -> 7.77 us
  local copies, waits for them, and re-layouts: 14.7 us -> 10.4 us
    unnamed x3 -> x0, waiting for transfers between devices: 60.2 us -> none
    all_to_all x1 -> x0, blocking collectives: 48.9 us -> none  [body(): lax.all_to_all(send_grad, 'grp', split_axis=0, concat_axis=0, tiled=True)]
    ppermute x0 -> x11, starting transfers between devices: none -> 44.1 us  [the longest x4 19.6 us: body(): near.append(move(near[-1], perm=ahead))]
    all_to_all x2 -> x3, starting transfers between devices: 18.8 us -> 42 us  [the longest x1 24 us: body(): lax.all_to_all(send.reshape(groups, SUB, -1), 'grp', split_axis=0, concat...]
    all_gather x1 -> x0, blocking collectives: 19.6 us -> none  [body(): lax.all_gather(lane_prob, 'loc', axis=0, tiled=True)]
    all_to_all x2 -> x3, waiting for transfers between devices: 20.5 us -> 35.2 us  [the longest x1 21 us: body(): lax.all_to_all(send.reshape(groups, SUB, -1), 'grp', split_axis=0, concat...]
    all_gather x1 -> x0, waiting for transfers between devices: 13.5 us -> none  [body(): lax.all_gather(lane_grad, 'loc', axis=0, tiled=True)]
    dot_general x7 -> x0, matrix products: 11.5 us -> none  [the longest x1 5.7 us: local_terms(): lax.dot_general(grad_rows, down_weight, (((1,), (1,)), ((), ())), preferr...]
  transfers between devices with their start and end apart: 4 -> 14, of which waited for: 4 -> 9; matrix products, arithmetic and copies ran while one was open for 1% -> 1% of each run, Pallas kernels for 0% -> 1%
where the time goes in v1:
time: 151 us; the launch traced here: 150 us
  starting transfers between devices  86.1 us (57%)
  waiting for transfers between devices  44.9 us (30%)
  local copies, waits for them, and re-layouts  10.4 us (7%)
  Pallas kernels  7.77 us (5%)
    all_to_all x1, starting transfers between devices, body(): lax.all_to_all(send.reshape(groups, SUB, -1), 'grp', split_axis=0, concat...  24 us
    all_to_all x1, waiting for transfers between devices, body(): lax.all_to_all(send.reshape(groups, SUB, -1), 'grp', split_axis=0, concat...  21 us
    ppermute x4, starting transfers between devices, body(): near.append(move(near[-1], perm=ahead))  19.6 us
    ppermute x3, starting transfers between devices, body(): far.append(move(far[-1], perm=ahead))  12.5 us
    all_to_all x1, starting transfers between devices, body(): parts = lax.all_to_all(sums, 'loc', split_axis=0, concat_axis=0, tiled=True)  11.9 us
    all_to_all x1, waiting for transfers between devices, body(): lax.all_to_all(jnp.broadcast_to(lane, (groups, 1, LANES)), 'grp', split_a...  9.34 us
    ppermute x4, waiting for transfers between devices, body(): near.append(move(near[-1], perm=ahead))  8.84 us
    pallas_call x4, Pallas kernels, call(): pl.pallas_call(kernel, in_specs=specs, out_specs=VMEM if single else [VME...  7.77 us
  transfers between devices with their start and end apart: 14, of which 9 were waited for; matrix products, arithmetic and copies ran while one was open for 1% of the time, Pallas kernels for 1%

profile of v1, /device:TPU:1, one launch (start us, length us, event | category | flops | bytes accessed | tf_op | source)
XLA Modules:
  0.0 150.4 jit_solution(1369099463881791740)
XLA Ops:
  0.6 0.8 copy.19
  1.4 0.7 tile.10
  2.1 0.1 tile.11.gid_ref
  2.2 0.0 copy-start.5
  2.2 0.0 copy-start.8
  2.2 0.1 copy.15.prob_ref
  2.4 0.0 copy-start.7
  2.4 0.9 copy-done.7
  3.3 1.6 %shard_map.68 = bf16[512,1024]{1,0:T(8,128)(2,1)} custom-call(bf16[8,7168]{1,0:T(8,128)(2,1)S(1)} %copy-done.7, s32[4,64]{1,0:T(4,128)S(1)} %tile.11.gid_ref, bf16[4,128,64]{2,1,0:T(8,128)(2,1)S(1)} %copy.15.prob_ref), custom_call_target="tpu_custom_call" | custom-call | tf_op jit(solution)/shard_map/pallas_call | solution.py:128
  4.8 24.0 %all-to-all-start = ((bf16[64,8,1024]{2,1,0:T(8,128)(2,1)}), bf16[64,8,1024]{2,1,0:T(8,128)(2,1)S(1)}, u32[]{:S(2)}, u32[]{:S(2)}) async-start(bf16[64,8,1024]{2,1,0:T(8,128)(2,1)} %bitcast.20), calls=%async_computation | async-start | bytes 2097152 | tf_op jit(solution)/shard_map/all_to_all | solution.py:173
  28.8 2.9 %collective-permute-start = (bf16[128,7168]{1,0:T(8,128)(2,1)}, bf16[128,7168]{1,0:T(8,128)(2,1)S(1)}, u32[]{:S(2)}, u32[]{:S(2)}) collective-permute-start(bf16[128,7168]{1,0:T(8,128)(2,1)} %refs_8_.1), channel_id=1, source_target_pairs={{0,1},{1,0},{2,3},{3,2},{4,5},{5,4},{6,7},{7,6},{8,9},{9,8},{10,11... | collective-permute-start | bytes 5505032 | tf_op jit(solution)/shard_map/ppermute | solution.py:178
  31.7 0.0 copy-done.5
  31.7 1.9 %collective-permute-start.1 = (bf16[512,128]{1,0:T(8,128)(2,1)S(1)}, bf16[512,128]{1,0:T(8,128)(2,1)S(1)}, u32[]{:S(2)}, u32[]{:S(2)}) collective-permute-start(bf16[512,128]{1,0:T(8,128)(2,1)S(1)} %bitcast.32), channel_id=1, source_target_pairs={{0,1},{1,0},{2,3},{3,2},{4,5},{5,4},{6,7},{7,6},{8,9},{9,8},{10,11... | collective-permute-start | bytes 393224 | tf_op jit(solution)/shard_map/ppermute | solution.py:179
  33.6 0.0 copy-done.8
  33.6 0.1 copy.16
  33.7 0.1 reshape.79
  33.8 0.8 add.204.source_ref
  34.6 0.6 collective-permute-done.1.refs_1_.refs_11_
  35.2 0.0 collective-permute-done.refs_0_.refs_9_
  35.3 0.0 copy-start
  35.3 21.0 %all-to-all-done = bf16[64,8,1024]{2,1,0:T(8,128)(2,1)S(1)} async-done(((bf16[64,8,1024]{2,1,0:T(8,128)(2,1)}), bf16[64,8,1024]{2,1,0:T(8,128)(2,1)S(1)}, u32[]{:S(2)}, u32[]{:S(2)}) %all-to-all-start) | async-done | bytes 1048608 | tf_op jit(solution)/shard_map/all_to_all | solution.py:173
  56.2 0.0 copy-start.2
  56.2 0.9 copy-done.2
  57.1 0.5 shard_map.69.refs_0_
  57.7 5.2 %collective-permute-start.6 = (bf16[264,896]{1,0:T(8,128)(2,1)S(1)}, bf16[264,896]{1,0:T(8,128)(2,1)S(1)}, u32[]{:S(2)}, u32[]{:S(2)}) collective-permute-start(bf16[264,896]{1,0:T(8,128)(2,1)S(1)} %shard_map.69.refs_0_), channel_id=1, source_target_pairs={{0,1},{1,0},{2,3},{3,2},{4,5},{5,4},{6,7},{7,6},{8,9},{9,8},{10,11... | collective-permute-start | bytes 1419272 | tf_op jit(solution)/shard_map/ppermute | solution.py:195
  62.9 4.5 %collective-permute-start.2 = (bf16[264,896]{1,0:T(8,128)(2,1)S(1)}, bf16[264,896]{1,0:T(8,128)(2,1)S(1)}, u32[]{:S(2)}, u32[]{:S(2)}) collective-permute-start(bf16[264,896]{1,0:T(8,128)(2,1)S(1)} %shard_map.69.refs_0_), channel_id=1, source_target_pairs={{0,2},{1,15},{2,4},{3,1},{4,6},{5,3},{6,8},{7,5},{8,10},{9,7},{10,... | collective-permute-start | bytes 1419272 | tf_op jit(solution)/shard_map/ppermute | solution.py:198
  67.4 0.0 collective-permute-done.6
  67.4 3.1 %collective-permute-start.7 = (bf16[264,896]{1,0:T(8,128)(2,1)S(1)}, bf16[264,896]{1,0:T(8,128)(2,1)S(1)}, u32[]{:S(2)}, u32[]{:S(2)}) collective-permute-start(bf16[264,896]{1,0:T(8,128)(2,1)S(1)} %collective-permute-done.6), channel_id=1, source_target_pairs={{0,2},{1,15},{2,4},{3,1},{4,6},{5,3},{6,8},{7,5},{8,10},{9,7},{10,... | collective-permute-start | bytes 1419272 | tf_op jit(solution)/shard_map/ppermute | solution.py:200
  70.5 2.5 %collective-permute-done.2.refs_1_ = bf16[264,896]{1,0:T(8,128)(2,1)S(1)} collective-permute-done((bf16[264,896]{1,0:T(8,128)(2,1)S(1)}, bf16[264,896]{1,0:T(8,128)(2,1)S(1)}, u32[]{:S(2)}, u32[]{:S(2)}) %collective-permute-start.2) | collective-permute-done | bytes 473120 | tf_op jit(solution)/shard_map/ppermute | solution.py:198
  73.0 5.0 %collective-permute-start.3 = (bf16[264,896]{1,0:T(8,128)(2,1)S(1)}, bf16[264,896]{1,0:T(8,128)(2,1)S(1)}, u32[]{:S(2)}, u32[]{:S(2)}) collective-permute-start(bf16[264,896]{1,0:T(8,128)(2,1)S(1)} %collective-permute-done.2.refs_1_), channel_id=1, source_target_pairs={{0,2},{1,15},{2,4},{3,1},{4,6},{5,3},{6,8},{7,5},{8,10},{9,7},{10,... | collective-permute-start | bytes 1419272 | tf_op jit(solution)/shard_map/ppermute | solution.py:198
  78.0 0.0 collective-permute-done.7.refs_5_
  78.0 5.0 %collective-permute-start.8 = (bf16[264,896]{1,0:T(8,128)(2,1)S(1)}, bf16[264,896]{1,0:T(8,128)(2,1)}, u32[]{:S(2)}, u32[]{:S(2)}) collective-permute-start(bf16[264,896]{1,0:T(8,128)(2,1)S(1)} %collective-permute-done.7.refs_5_), channel_id=1, source_target_pairs={{0,2},{1,15},{2,4},{3,1},{4,6},{5,3},{6,8},{7,5},{8,10},{9,7},{10,... | collective-permute-start | bytes 1419272 | tf_op jit(solution)/shard_map/ppermute | solution.py:200
  83.1 0.5 collective-permute-done.3.refs_2_
  83.5 5.0 %collective-permute-start.4 = (bf16[264,896]{1,0:T(8,128)(2,1)S(1)}, bf16[264,896]{1,0:T(8,128)(2,1)}, u32[]{:S(2)}, u32[]{:S(2)}) collective-permute-start(bf16[264,896]{1,0:T(8,128)(2,1)S(1)} %collective-permute-done.3.refs_2_), channel_id=1, source_target_pairs={{0,2},{1,15},{2,4},{3,1},{4,6},{5,3},{6,8},{7,5},{8,10},{9,7},{10,... | collective-permute-start | bytes 1419272 | tf_op jit(solution)/shard_map/ppermute | solution.py:198
  88.6 0.0 copy-start.3
  88.6 0.8 copy-done.3
  89.3 0.0 collective-permute-done.8.refs_6_
  89.3 4.4 %collective-permute-start.9 = (bf16[264,896]{1,0:T(8,128)(2,1)}, bf16[264,896]{1,0:T(8,128)(2,1)}, u32[]{:S(2)}, u32[]{:S(2)}) collective-permute-start(bf16[264,896]{1,0:T(8,128)(2,1)} %collective-permute-done.8.refs_6_), channel_id=1, source_target_pairs={{0,2},{1,15},{2,4},{3,1},{4,6},{5,3},{6,8},{7,5},{8,10},{9,7},{10,... | collective-permute-start | bytes 1419272 | tf_op jit(solution)/shard_map/ppermute | solution.py:200
  93.7 0.4 collective-permute-done.4.refs_3_
  94.1 5.1 %collective-permute-start.5 = (bf16[264,896]{1,0:T(8,128)(2,1)}, bf16[264,896]{1,0:T(8,128)(2,1)}, u32[]{:S(2)}, u32[]{:S(2)}) collective-permute-start(bf16[264,896]{1,0:T(8,128)(2,1)} %collective-permute-done.4.refs_3_), channel_id=1, source_target_pairs={{0,2},{1,15},{2,4},{3,1},{4,6},{5,3},{6,8},{7,5},{8,10},{9,7},{10,... | collective-permute-start | bytes 1419272 | tf_op jit(solution)/shard_map/ppermute | solution.py:198
  99.3 0.0 copy-done
  99.4 0.1 concatenate.3.place_ref
  99.5 0.2 collective-permute-done.9.refs_7_
  99.6 5.5 %collective-permute-done.5.refs_4_ = bf16[264,896]{1,0:T(8,128)(2,1)} collective-permute-done((bf16[264,896]{1,0:T(8,128)(2,1)}, bf16[264,896]{1,0:T(8,128)(2,1)}, u32[]{:S(2)}, u32[]{:S(2)}) %collective-permute-start.5) | collective-permute-done | bytes 473120 | tf_op jit(solution)/shard_map/ppermute | solution.py:198
  105.1 0.0 copy-start.1
  105.1 1.5 copy-done.1
  106.6 0.0 copy-start.4
  106.6 1.0 copy-done.4
  107.6 0.0 copy-start.6
  107.6 0.9 copy-done.6
  108.5 4.4 %shard_map.70 = (bf16[512,128]{1,0:T(8,128)(2,1)S(1)}, bf16[256,128]{1,0:T(8,128)(2,1)S(1)}, f32[16,1,128]{2,1,0:T(1,128)}) custom-call(s32[9]{0:T(128)S(1)} %concatenate.3.place_ref, bf16[264,896]{1,0:T(8,128)(2,1)S(1)} %shard_map.69.refs_0_, bf16[264,896]{1,0:T(8,128)(2,1)S(1)} %collective-permute-done.2.refs_1_, bf16[264,896]{1,0:T(8,128)(2,1)S(1)} %copy-done.4, ...), custom_call_target="tpu_custom_call" | custom-call | tf_op jit(solution)/shard_map/pallas_call | solution.py:128
  113.0 11.9 %all-to-all-start.1 = ((f32[16,1,128]{2,1,0:T(1,128)}), f32[16,1,128]{2,1,0:T(1,128)S(1)}, u32[]{:S(2)}, u32[]{:S(2)}) async-start(f32[16,1,128]{2,1,0:T(1,128)} %get-tuple-element.7), calls=%async_computation.1 | async-start | bytes 16384 | tf_op jit(solution)/shard_map/all_to_all | solution.py:227
  124.9 2.0 %collective-permute-start.10 = (bf16[256,128]{1,0:T(8,128)(2,1)S(1)}, bf16[256,128]{1,0:T(8,128)(2,1)S(1)}, u32[]{:S(2)}, u32[]{:S(2)}) collective-permute-start(bf16[256,128]{1,0:T(8,128)(2,1)S(1)} %get-tuple-element.6), channel_id=1, source_target_pairs={{0,1},{1,0},{2,3},{3,2},{4,5},{5,4},{6,7},{7,6},{8,9},{9,8},{10,11... | collective-permute-start | bytes 196616 | tf_op jit(solution)/shard_map/ppermute | solution.py:226
  126.9 4.9 %all-to-all-done.1 = f32[16,1,128]{2,1,0:T(1,128)S(1)} async-done(((f32[16,1,128]{2,1,0:T(1,128)}), f32[16,1,128]{2,1,0:T(1,128)S(1)}, u32[]{:S(2)}, u32[]{:S(2)}) %all-to-all-start.1) | async-done | bytes 8224 | tf_op jit(solution)/shard_map/all_to_all | solution.py:227
  131.9 0.1 reshape.81
  131.9 0.6 broadcast_in_dim.14
  132.6 6.1 %all-to-all-start.2 = ((f32[64,1,128]{2,1,0:T(1,128)}), f32[64,1,128]{2,1,0:T(1,128)S(1)}, u32[]{:S(2)}, u32[]{:S(2)}) async-start(f32[64,1,128]{2,1,0:T(1,128)} %broadcast_in_dim.14), calls=%async_computation.2 | async-start | bytes 65536 | tf_op jit(solution)/shard_map/all_to_all | solution.py:230
  138.8 0.1 eq.36
  138.9 0.1 stack.59.place_ref
  139.0 0.0 collective-permute-done.10.got_ref
  139.0 1.2 shard_map.71
  140.2 9.3 %all-to-all-done.2 = f32[64,1,128]{2,1,0:T(1,128)S(1)} async-done(((f32[64,1,128]{2,1,0:T(1,128)}), f32[64,1,128]{2,1,0:T(1,128)S(1)}, u32[]{:S(2)}, u32[]{:S(2)}) %all-to-all-start.2) | async-done | bytes 32800 | tf_op jit(solution)/shard_map/all_to_all | solution.py:230
  149.6 0.1 reshape.82
  149.7 0.7 copy.18
  (8 shorter events, 0.1 us)
Async XLA Ops:
  2.2 29.5 %copy-start.5 = (bf16[1,512,128]{2,1,0:T(8,128)(2,1)S(1)}, bf16[1,512,128]{2,1,0:T(8,128)(2,1)}, u32[]{:S(2)}) copy-start(bf16[1,512,128]{2,1,0:T(8,128)(2,1)} %param.8) | copy-start | bytes 393220
  2.2 31.4 %copy-start.8 = (s32[8,4]{0,1:T(4,128)S(1)}, s32[8,4]{0,1:T(4,128)}, u32[]{:S(2)}) copy-start(s32[8,4]{0,1:T(4,128)} %param.7) | copy-start | bytes 388
  2.4 0.9 copy-start.7
  4.8 51.4 %all-to-all-start = ((bf16[64,8,1024]{2,1,0:T(8,128)(2,1)}), bf16[64,8,1024]{2,1,0:T(8,128)(2,1)S(1)}, u32[]{:S(2)}, u32[]{:S(2)}) async-start(bf16[64,8,1024]{2,1,0:T(8,128)(2,1)} %bitcast.20), calls=%async_computation | async-start | bytes 2097152 | tf_op jit(solution)/shard_map/all_to_all | solution.py:173
  28.8 6.5 %collective-permute-start = (bf16[128,7168]{1,0:T(8,128)(2,1)}, bf16[128,7168]{1,0:T(8,128)(2,1)S(1)}, u32[]{:S(2)}, u32[]{:S(2)}) collective-permute-start(bf16[128,7168]{1,0:T(8,128)(2,1)} %refs_8_.1), channel_id=1, source_target_pairs={{0,1},{1,0},{2,3},{3,2},{4,5},{5,4},{6,7},{7,6},{8,9},{9,8},{10,11... | collective-permute-start | bytes 5505032 | tf_op jit(solution)/shard_map/ppermute | solution.py:178
  31.7 3.6 %collective-permute-start.1 = (bf16[512,128]{1,0:T(8,128)(2,1)S(1)}, bf16[512,128]{1,0:T(8,128)(2,1)S(1)}, u32[]{:S(2)}, u32[]{:S(2)}) collective-permute-start(bf16[512,128]{1,0:T(8,128)(2,1)S(1)} %bitcast.32), channel_id=1, source_target_pairs={{0,1},{1,0},{2,3},{3,2},{4,5},{5,4},{6,7},{7,6},{8,9},{9,8},{10,11... | collective-permute-start | bytes 393224 | tf_op jit(solution)/shard_map/ppermute | solution.py:179
  35.3 64.0 %copy-start = (bf16[128,7168]{1,0:T(8,128)(2,1)}, bf16[128,7168]{1,0:T(8,128)(2,1)S(1)}, u32[]{:S(2)}) copy-start(bf16[128,7168]{1,0:T(8,128)(2,1)S(1)} %collective-permute-done.refs_0_.refs_9_) | copy-start | bytes 5505028
  56.2 0.9 copy-start.2
  57.7 9.7 %collective-permute-start.6 = (bf16[264,896]{1,0:T(8,128)(2,1)S(1)}, bf16[264,896]{1,0:T(8,128)(2,1)S(1)}, u32[]{:S(2)}, u32[]{:S(2)}) collective-permute-start(bf16[264,896]{1,0:T(8,128)(2,1)S(1)} %shard_map.69.refs_0_), channel_id=1, source_target_pairs={{0,1},{1,0},{2,3},{3,2},{4,5},{5,4},{6,7},{7,6},{8,9},{9,8},{10,11... | collective-permute-start | bytes 1419272 | tf_op jit(solution)/shard_map/ppermute | solution.py:195
  62.9 10.1 %collective-permute-start.2 = (bf16[264,896]{1,0:T(8,128)(2,1)S(1)}, bf16[264,896]{1,0:T(8,128)(2,1)S(1)}, u32[]{:S(2)}, u32[]{:S(2)}) collective-permute-start(bf16[264,896]{1,0:T(8,128)(2,1)S(1)} %shard_map.69.refs_0_), channel_id=1, source_target_pairs={{0,2},{1,15},{2,4},{3,1},{4,6},{5,3},{6,8},{7,5},{8,10},{9,7},{10,... | collective-permute-start | bytes 1419272 | tf_op jit(solution)/shard_map/ppermute | solution.py:198
  67.4 10.6 %collective-permute-start.7 = (bf16[264,896]{1,0:T(8,128)(2,1)S(1)}, bf16[264,896]{1,0:T(8,128)(2,1)S(1)}, u32[]{:S(2)}, u32[]{:S(2)}) collective-permute-start(bf16[264,896]{1,0:T(8,128)(2,1)S(1)} %collective-permute-done.6), channel_id=1, source_target_pairs={{0,2},{1,15},{2,4},{3,1},{4,6},{5,3},{6,8},{7,5},{8,10},{9,7},{10,... | collective-permute-start | bytes 1419272 | tf_op jit(solution)/shard_map/ppermute | solution.py:200
  73.0 10.6 %collective-permute-start.3 = (bf16[264,896]{1,0:T(8,128)(2,1)S(1)}, bf16[264,896]{1,0:T(8,128)(2,1)S(1)}, u32[]{:S(2)}, u32[]{:S(2)}) collective-permute-start(bf16[264,896]{1,0:T(8,128)(2,1)S(1)} %collective-permute-done.2.refs_1_), channel_id=1, source_target_pairs={{0,2},{1,15},{2,4},{3,1},{4,6},{5,3},{6,8},{7,5},{8,10},{9,7},{10,... | collective-permute-start | bytes 1419272 | tf_op jit(solution)/shard_map/ppermute | solution.py:198
  78.0 11.3 %collective-permute-start.8 = (bf16[264,896]{1,0:T(8,128)(2,1)S(1)}, bf16[264,896]{1,0:T(8,128)(2,1)}, u32[]{:S(2)}, u32[]{:S(2)}) collective-permute-start(bf16[264,896]{1,0:T(8,128)(2,1)S(1)} %collective-permute-done.7.refs_5_), channel_id=1, source_target_pairs={{0,2},{1,15},{2,4},{3,1},{4,6},{5,3},{6,8},{7,5},{8,10},{9,7},{10,... | collective-permute-start | bytes 1419272 | tf_op jit(solution)/shard_map/ppermute | solution.py:200
  83.5 10.6 %collective-permute-start.4 = (bf16[264,896]{1,0:T(8,128)(2,1)S(1)}, bf16[264,896]{1,0:T(8,128)(2,1)}, u32[]{:S(2)}, u32[]{:S(2)}) collective-permute-start(bf16[264,896]{1,0:T(8,128)(2,1)S(1)} %collective-permute-done.3.refs_2_), channel_id=1, source_target_pairs={{0,2},{1,15},{2,4},{3,1},{4,6},{5,3},{6,8},{7,5},{8,10},{9,7},{10,... | collective-permute-start | bytes 1419272 | tf_op jit(solution)/shard_map/ppermute | solution.py:198
  88.6 0.8 copy-start.3
  89.3 10.3 %collective-permute-start.9 = (bf16[264,896]{1,0:T(8,128)(2,1)}, bf16[264,896]{1,0:T(8,128)(2,1)}, u32[]{:S(2)}, u32[]{:S(2)}) collective-permute-start(bf16[264,896]{1,0:T(8,128)(2,1)} %collective-permute-done.8.refs_6_), channel_id=1, source_target_pairs={{0,2},{1,15},{2,4},{3,1},{4,6},{5,3},{6,8},{7,5},{8,10},{9,7},{10,... | collective-permute-start | bytes 1419272 | tf_op jit(solution)/shard_map/ppermute | solution.py:200
  94.1 11.0 %collective-permute-start.5 = (bf16[264,896]{1,0:T(8,128)(2,1)}, bf16[264,896]{1,0:T(8,128)(2,1)}, u32[]{:S(2)}, u32[]{:S(2)}) collective-permute-start(bf16[264,896]{1,0:T(8,128)(2,1)} %collective-permute-done.4.refs_3_), channel_id=1, source_target_pairs={{0,2},{1,15},{2,4},{3,1},{4,6},{5,3},{6,8},{7,5},{8,10},{9,7},{10,... | collective-permute-start | bytes 1419272 | tf_op jit(solution)/shard_map/ppermute | solution.py:198
  105.1 1.5 copy-start.1
  106.6 1.0 copy-start.4
  107.6 0.9 copy-start.6
  113.0 18.9 %all-to-all-start.1 = ((f32[16,1,128]{2,1,0:T(1,128)}), f32[16,1,128]{2,1,0:T(1,128)S(1)}, u32[]{:S(2)}, u32[]{:S(2)}) async-start(f32[16,1,128]{2,1,0:T(1,128)} %get-tuple-element.7), calls=%async_computation.1 | async-start | bytes 16384 | tf_op jit(solution)/shard_map/all_to_all | solution.py:227
  124.9 14.1 %collective-permute-start.10 = (bf16[256,128]{1,0:T(8,128)(2,1)S(1)}, bf16[256,128]{1,0:T(8,128)(2,1)S(1)}, u32[]{:S(2)}, u32[]{:S(2)}) collective-permute-start(bf16[256,128]{1,0:T(8,128)(2,1)S(1)} %get-tuple-element.6), channel_id=1, source_target_pairs={{0,1},{1,0},{2,3},{3,2},{4,5},{5,4},{6,7},{7,6},{8,9},{9,8},{10,11... | collective-permute-start | bytes 196616 | tf_op jit(solution)/shard_map/ppermute | solution.py:226
  132.6 17.0 %all-to-all-start.2 = ((f32[64,1,128]{2,1,0:T(1,128)}), f32[64,1,128]{2,1,0:T(1,128)S(1)}, u32[]{:S(2)}, u32[]{:S(2)}) async-start(f32[64,1,128]{2,1,0:T(1,128)} %broadcast_in_dim.14), calls=%async_computation.2 | async-start | bytes 65536 | tf_op jit(solution)/shard_map/all_to_all | solution.py:230

commit v2 on v1

v2 whole, which is shorter than its diff:
```python
import functools

import jax
import jax.numpy as jnp
from jax import lax
from jax.experimental import pallas as pl
from jax.experimental.pallas import tpu as pltpu
from jax.sharding import PartitionSpec as P

SUB = 8
LANES = 128
NT = (((1,), (1,)), ((), ()))
TN = (((0,), (0,)), ((), ()))
BF = jnp.bfloat16
F32 = jnp.float32


def iota(shape, dim):
    return lax.broadcasted_iota(jnp.int32, shape, dim)


def send_kernel(grad_ref, gid_ref, prob_ref, out_ref):
    tok = grad_ref.shape[0]
    rows = out_ref.shape[0]
    wide = grad_ref.shape[1] // SUB
    slot = iota((rows, tok), 0) // SUB
    pick = jnp.zeros((rows, tok), F32)
    prob = jnp.zeros((rows, prob_ref.shape[1]), F32)
    for k in range(gid_ref.shape[0]):
        here = jnp.where(slot == gid_ref[k : k + 1, :], 1.0, 0.0)
        pick += here
        prob += lax.dot_general(here.astype(BF), prob_ref[k], NT, preferred_element_type=F32)
    dims = (tok, SUB * tok)
    spread = jnp.where(iota(dims, 1) % tok == iota(dims, 0), 1.0, 0.0).astype(BF)
    pick = jnp.dot(pick.astype(BF), spread, preferred_element_type=F32)
    dims = pick.shape
    pick = jnp.where(iota(dims, 0) % SUB == iota(dims, 1) // tok, pick, 0.0)
    dims = (prob.shape[1], LANES)
    spread = jnp.where(iota(dims, 0) == iota(dims, 1), 1.0, 0.0).astype(BF)
    prob = jnp.dot(prob.astype(BF), spread, preferred_element_type=F32)
    grad = jnp.concatenate([grad_ref[:, e * wide : (e + 1) * wide] for e in range(SUB)], axis=0)
    out_ref[:, :wide] = jnp.dot(pick.astype(BF), grad, preferred_element_type=F32).astype(BF)
    out_ref[:, wide:] = prob.astype(BF)


def pick_kernel(group_ref, recv_ref, gid_ref, *refs):
    out_ref = refs[-1]
    top, tok = gid_ref.shape
    lane_rows = top * tok
    rows = SUB * lane_rows
    wide = out_ref.shape[1]
    slots = recv_ref.shape[0]
    dims = (rows, tok)
    spread = jnp.where(iota(dims, 0) % lane_rows // top == iota(dims, 1), 1.0, 0.0).astype(BF)
    gids = lax.dot_general(
        spread, gid_ref[...].astype(F32).astype(BF), NT, preferred_element_type=F32
    )
    dims = (rows, top)
    gids = jnp.sum(jnp.where(iota(dims, 0) % top == iota(dims, 1), gids, 0.0), axis=1, keepdims=True)
    source = 2 * group_ref[0] - gids.astype(jnp.int32)
    groups = slots // SUB
    source = jnp.where(source < 0, source + groups, source)
    source = jnp.where(source >= groups, source - groups, source)
    source = source * SUB + iota((rows, 1), 0) // lane_rows
    pick = jnp.where(iota((rows, slots), 1) == source, 1.0, 0.0).astype(BF)
    out_ref[:rows, :] = jnp.dot(pick, recv_ref[:, :wide], preferred_element_type=F32).astype(BF)
    prob = jnp.dot(pick[:lane_rows], recv_ref[:, wide:], preferred_element_type=F32)
    prob = jnp.transpose(prob)[:SUB]
    pad = jnp.zeros((SUB, wide - lane_rows), F32)
    out_ref[rows:, :] = jnp.concatenate([prob, pad], axis=1).astype(BF)


def terms_kernel(place_ref, *refs):
    shards, last_prob = refs[:-8], refs[-8]
    own_w, mate_w, own_gate, mate_gate, pre_ref, give_ref, sum_ref = refs[-7:]
    count = len(shards)
    rows = (shards[0].shape[0] - SUB) // SUB
    width, model = own_w.shape
    wide = model // SUB
    hidden = jnp.zeros((count * rows, 2 * width), F32)
    for e in range(SUB):
        left = jnp.concatenate([ref[e * rows : (e + 1) * rows, :] for ref in shards], axis=0)
        cols = slice(e * wide, (e + 1) * wide)
        right = jnp.concatenate([own_w[:, cols], mate_w[:, cols]], axis=0)
        hidden += lax.dot_general(left, right, NT, preferred_element_type=F32)
    expert = jnp.where(iota((SUB, width), 0) == place_ref[count], 1.0, 0.0).astype(BF)
    terms = []
    for i, ref in enumerate(shards):
        at = pl.ds(pl.multiple_of(place_ref[i] * rows, rows), rows)
        prob = last_prob[...] if i == count - 1 else ref[SUB * rows :, :]
        scale = lax.dot_general(
            prob[:, :rows], expert, TN, preferred_element_type=F32
        )
        total = jnp.zeros((rows, width), F32)
        for half, gate in enumerate((own_gate, mate_gate)):
            grad = hidden[i * rows : (i + 1) * rows, half * width : (half + 1) * width]
            value = gate[at, :].astype(F32)
            sigma = jax.nn.sigmoid(value)
            slope = sigma * (1.0 + value * (1.0 - sigma))
            total += value * sigma * grad
            result = (scale * grad * slope).astype(BF)
            if half == 0:
                pre_ref[at, :] = result
            else:
                give_ref[i * rows : (i + 1) * rows, :] = result
        terms.append(total)
    sums = lax.dot_general(
        jnp.ones((SUB, width), F32),
        jnp.concatenate(terms, axis=0),
        NT,
        precision=lax.Precision.HIGHEST,
        preferred_element_type=F32,
    )
    sum_ref[...] = jnp.zeros(sum_ref.shape, F32)
    for i in range(count):
        sum_ref[pl.ds(place_ref[i], 1), 0, :rows] = sums[:1, i * rows : (i + 1) * rows]


def prob_kernel(shard_ref, out_ref):
    out_ref[...] = shard_ref[shard_ref.shape[0] - SUB :, :]


def join_kernel(place_ref, half_ref, got_ref, out_ref):
    rows = got_ref.shape[0] // place_ref.shape[0]
    out_ref[...] = half_ref[...]
    for i in range(place_ref.shape[0]):
        at = pl.ds(pl.multiple_of(place_ref[i] * rows, rows), rows)
        out_ref[at, :] = got_ref[i * rows : (i + 1) * rows, :]


BLOCK = pl.BlockSpec()
VMEM = pl.BlockSpec(memory_space=pltpu.VMEM)
SMEM = pl.BlockSpec(memory_space=pltpu.SMEM)
ANY = pl.BlockSpec(memory_space=pl.ANY)
PARAMS = pltpu.CompilerParams(vmem_limit_bytes=12 * 1024 * 1024)


def hbm(*arrays):
    return [pltpu.with_memory_space_constraint(one, pltpu.HBM) for one in arrays]


def call(kernel, specs, shapes, *args):
    return pl.pallas_call(
        kernel, in_specs=specs, out_shape=shapes, compiler_params=PARAMS
    )(*args)


def shape(dims, kind):
    return jax.ShapeDtypeStruct(dims, kind)


def body(out_grad, route_prob, group_ids, gate_pre, down_weight):
    tok, model = out_grad.shape
    top = group_ids.shape[1]
    experts = route_prob.shape[2]
    groups = lax.axis_size("grp")
    locs = lax.axis_size("loc")
    chips = locs // 2
    rows = tok * top
    gate_rows = gate_pre[0]
    width = gate_rows.shape[1]
    my_group = lax.axis_index("grp")
    loc = lax.axis_index("loc")
    swap = [(l, l ^ 1) for l in range(locs)]
    ahead = [(l, (l + (2 if l % 2 == 0 else -2)) % locs) for l in range(locs)]

    gid = group_ids.T
    prob = jnp.transpose(route_prob, (1, 2, 0))
    wide = model // SUB
    send = call(
        send_kernel, [BLOCK] * 3, shape((groups * SUB, wide + LANES), BF), *hbm(out_grad, gid, prob)
    )
    move = functools.partial(lax.ppermute, axis_name="loc")
    recv = lax.all_to_all(
        send.reshape(groups, SUB, -1), "grp", split_axis=0, concat_axis=0, tiled=True
    ).reshape(groups * SUB, -1)
    mate_w = move(down_weight, perm=swap)
    mate_gate = move(gate_rows, perm=swap)
    own = call(
        pick_kernel,
        [SMEM, BLOCK, BLOCK, ANY, ANY],
        shape((SUB * rows + SUB, wide), BF),
        my_group.reshape(1),
        recv,
        gid,
        mate_w,
        mate_gate,
    )
    near, far = [own], [move(own, perm=swap)]
    for step in range(chips // 2):
        near.append(move(near[-1], perm=ahead))
        if step < chips // 2 - 1:
            far.append(move(far[-1], perm=ahead))
    shards = near + far[1:]
    count = len(shards)

    def places(at):
        chip, core = at // 2, at % 2
        step = 2 * core - 1
        hops = [(k, core) for k in range(chips // 2 + 1)] + [(k, 1 - core) for k in range(1, chips // 2)]
        return jnp.stack([(chip + step * k) % chips * 2 + c for k, c in hops]).astype(jnp.int32)

    place = jnp.concatenate([places(loc), (loc // (locs // experts)).reshape(1)])
    last_prob = call(prob_kernel, [VMEM], shape((SUB, wide), BF), far[-1])
    half, give, sums = call(
        terms_kernel,
        [SMEM] + [VMEM] * (count + 5),
        [
            shape(gate_rows.shape, BF),
            shape((count * rows, width), BF),
            shape((locs, 1, LANES), F32),
        ],
        place,
        *shards,
        last_prob,
        down_weight,
        mate_w,
        gate_rows,
        mate_gate,
    )
    got = move(give, perm=swap)
    parts = lax.all_to_all(sums, "loc", split_axis=0, concat_axis=0, tiled=True)
    lane = jnp.sum(parts.reshape(experts, locs // experts, LANES), axis=1)
    lane = jnp.pad(lane[:, :rows].reshape(experts * rows), (0, LANES - experts * rows))
    back = lax.all_to_all(
        jnp.broadcast_to(lane, (groups, 1, LANES)), "grp", split_axis=0, concat_axis=0, tiled=True
    )[:, 0]
    pre = call(join_kernel, [SMEM, BLOCK, BLOCK], shape(gate_rows.shape, BF), places(loc ^ 1), *hbm(half), got)
    flat = group_ids.reshape(rows)
    wanted = jnp.tile(flat, experts)[None, :] == jnp.arange(groups, dtype=jnp.int32)[:, None]
    route = jnp.sum(jnp.where(wanted, back[:, : experts * rows], 0.0), axis=0)
    route = jnp.transpose(route.reshape(experts, tok, top), (1, 2, 0))
    return pre[None], route


def solution(mesh):
    placed = (
        P(("grp", "loc"), None),
        P(("grp", "loc"), None, None),
        P(("grp", "loc"), None),
        P("grp", None, "loc"),
        P(("grp", "loc"), None),
    )
    return jax.shard_map(
        body,
        mesh=mesh,
        in_specs=placed,
        out_specs=(P("grp", None, "loc"), P(("grp", "loc"), None, None)),
        check_vma=False,
    )
```

time: 151 us -> 150 us (level)
  local copies, waits for them, and re-layouts: 10.4 us -> 8.55 us
    pallas_call x4 -> x5, Pallas kernels: 7.77 us -> 8.76 us  [call(): pl.pallas_call(kernel, in_specs=specs, out_shape=shapes, compiler_params=...]
    unnamed x21 -> x20, local copies, waits for them, and re-layouts: 7.58 us -> 7.42 us
  transfers between devices with their start and end apart: 14 -> 14, of which waited for: 9 -> 8; matrix products, arithmetic and copies ran while one was open for 1% -> 1% of each run, Pallas kernels for 1% -> 1%
where the time goes in v2:
time: 150 us; the launch traced here: 149 us
  starting transfers between devices  85.8 us (57%)
  waiting for transfers between devices  44.9 us (30%)
  Pallas kernels  8.76 us (6%)
  local copies, waits for them, and re-layouts  8.55 us (6%)
    all_to_all x1, starting transfers between devices, body(): lax.all_to_all(send.reshape(groups, SUB, -1), 'grp', split_axis=0, concat...  24 us
    all_to_all x1, waiting for transfers between devices, body(): lax.all_to_all(send.reshape(groups, SUB, -1), 'grp', split_axis=0, concat...  21 us
    ppermute x4, starting transfers between devices, body(): near.append(move(near[-1], perm=ahead))  19.4 us
    ppermute x3, starting transfers between devices, body(): far.append(move(far[-1], perm=ahead))  12.4 us
    all_to_all x1, starting transfers between devices, body(): parts = lax.all_to_all(sums, 'loc', split_axis=0, concat_axis=0, tiled=True)  11.9 us
    all_to_all x1, waiting for transfers between devices, body(): lax.all_to_all(jnp.broadcast_to(lane, (groups, 1, LANES)), 'grp', split_a...  8.79 us
    pallas_call x5, Pallas kernels, call(): pl.pallas_call(kernel, in_specs=specs, out_shape=shapes, compiler_params=...  8.76 us
    ppermute x4, waiting for transfers between devices, body(): near.append(move(near[-1], perm=ahead))  8.37 us
  transfers between devices with their start and end apart: 14, of which 8 were waited for; matrix products, arithmetic and copies ran while one was open for 1% of the time, Pallas kernels for 1%

profile of v2, /device:TPU:1, one launch (start us, length us, event | category | flops | bytes accessed | tf_op | source)
XLA Modules:
  0.0 149.1 jit_solution(4017728934036919710)
XLA Ops:
  0.6 0.0 copy-start.8
  0.6 0.0 copy-start.5
  0.7 2.8 %shard_map.68 = bf16[512,1024]{1,0:T(8,128)(2,1)} custom-call(bf16[8,7168]{1,0:T(8,128)(2,1)} %grad_ref.1, s32[4,8]{1,0:T(4,128)} %bitcast.33, bf16[4,2,8]{2,1,0:T(2,128)(2,1)} %bitcast.39), custom_call_target="tpu_custom_call" | custom-call | tf_op jit(solution)/shard_map/pallas_call | solution.py:143
  3.5 24.0 %all-to-all-start = ((bf16[64,8,1024]{2,1,0:T(8,128)(2,1)}), bf16[64,8,1024]{2,1,0:T(8,128)(2,1)S(1)}, u32[]{:S(2)}, u32[]{:S(2)}) async-start(bf16[64,8,1024]{2,1,0:T(8,128)(2,1)} %bitcast.20), calls=%async_computation | async-start | bytes 2097152 | tf_op jit(solution)/shard_map/all_to_all | solution.py:174
  27.4 2.9 %collective-permute-start = (bf16[128,7168]{1,0:T(8,128)(2,1)}, bf16[128,7168]{1,0:T(8,128)(2,1)S(1)}, u32[]{:S(2)}, u32[]{:S(2)}) collective-permute-start(bf16[128,7168]{1,0:T(8,128)(2,1)} %refs_9_.1), channel_id=1, source_target_pairs={{0,1},{1,0},{2,3},{3,2},{4,5},{5,4},{6,7},{7,6},{8,9},{9,8},{10,11... | collective-permute-start | bytes 5505032 | tf_op jit(solution)/shard_map/ppermute | solution.py:177
  30.3 0.0 copy-done.5
  30.3 1.9 %collective-permute-start.1 = (bf16[512,128]{1,0:T(8,128)(2,1)S(1)}, bf16[512,128]{1,0:T(8,128)(2,1)S(1)}, u32[]{:S(2)}, u32[]{:S(2)}) collective-permute-start(bf16[512,128]{1,0:T(8,128)(2,1)S(1)} %bitcast.31), channel_id=1, source_target_pairs={{0,1},{1,0},{2,3},{3,2},{4,5},{5,4},{6,7},{7,6},{8,9},{9,8},{10,11... | collective-permute-start | bytes 393224 | tf_op jit(solution)/shard_map/ppermute | solution.py:178
  32.2 1.6 %collective-permute-done.1.refs_1_.refs_12_ = bf16[512,128]{1,0:T(8,128)(2,1)S(1)} collective-permute-done((bf16[512,128]{1,0:T(8,128)(2,1)S(1)}, bf16[512,128]{1,0:T(8,128)(2,1)S(1)}, u32[]{:S(2)}, u32[]{:S(2)}) %collective-permute-start.1) | collective-permute-done | bytes 131104 | tf_op jit(solution)/shard_map/ppermute | solution.py:178
  33.9 0.0 collective-permute-done.refs_0_.refs_10_
  33.9 21.0 %all-to-all-done = bf16[64,8,1024]{2,1,0:T(8,128)(2,1)S(1)} async-done(((bf16[64,8,1024]{2,1,0:T(8,128)(2,1)}), bf16[64,8,1024]{2,1,0:T(8,128)(2,1)S(1)}, u32[]{:S(2)}, u32[]{:S(2)}) %all-to-all-start) | async-done | bytes 1048608 | tf_op jit(solution)/shard_map/all_to_all | solution.py:174
  54.9 0.0 copy-done.8
  54.9 0.7 shard_map.69.refs_0_
  55.6 5.2 %collective-permute-start.6 = (bf16[264,896]{1,0:T(8,128)(2,1)S(1)}, bf16[264,896]{1,0:T(8,128)(2,1)S(1)}, u32[]{:S(2)}, u32[]{:S(2)}) collective-permute-start(bf16[264,896]{1,0:T(8,128)(2,1)S(1)} %shard_map.69.refs_0_), channel_id=1, source_target_pairs={{0,1},{1,0},{2,3},{3,2},{4,5},{5,4},{6,7},{7,6},{8,9},{9,8},{10,11... | collective-permute-start | bytes 1419272 | tf_op jit(solution)/shard_map/ppermute | solution.py:189
  60.8 4.5 %collective-permute-start.2 = (bf16[264,896]{1,0:T(8,128)(2,1)S(1)}, bf16[264,896]{1,0:T(8,128)(2,1)S(1)}, u32[]{:S(2)}, u32[]{:S(2)}) collective-permute-start(bf16[264,896]{1,0:T(8,128)(2,1)S(1)} %shard_map.69.refs_0_), channel_id=1, source_target_pairs={{0,2},{1,15},{2,4},{3,1},{4,6},{5,3},{6,8},{7,5},{8,10},{9,7},{10,... | collective-permute-start | bytes 1419272 | tf_op jit(solution)/shard_map/ppermute | solution.py:191
  65.3 0.0 collective-permute-done.6
  65.3 3.1 %collective-permute-start.7 = (bf16[264,896]{1,0:T(8,128)(2,1)S(1)}, bf16[264,896]{1,0:T(8,128)(2,1)S(1)}, u32[]{:S(2)}, u32[]{:S(2)}) collective-permute-start(bf16[264,896]{1,0:T(8,128)(2,1)S(1)} %collective-permute-done.6), channel_id=1, source_target_pairs={{0,2},{1,15},{2,4},{3,1},{4,6},{5,3},{6,8},{7,5},{8,10},{9,7},{10,... | collective-permute-start | bytes 1419272 | tf_op jit(solution)/shard_map/ppermute | solution.py:193
  68.4 2.5 %collective-permute-done.2.refs_1_ = bf16[264,896]{1,0:T(8,128)(2,1)S(1)} collective-permute-done((bf16[264,896]{1,0:T(8,128)(2,1)S(1)}, bf16[264,896]{1,0:T(8,128)(2,1)S(1)}, u32[]{:S(2)}, u32[]{:S(2)}) %collective-permute-start.2) | collective-permute-done | bytes 473120 | tf_op jit(solution)/shard_map/ppermute | solution.py:191
  70.8 5.0 %collective-permute-start.3 = (bf16[264,896]{1,0:T(8,128)(2,1)S(1)}, bf16[264,896]{1,0:T(8,128)(2,1)S(1)}, u32[]{:S(2)}, u32[]{:S(2)}) collective-permute-start(bf16[264,896]{1,0:T(8,128)(2,1)S(1)} %collective-permute-done.2.refs_1_), channel_id=1, source_target_pairs={{0,2},{1,15},{2,4},{3,1},{4,6},{5,3},{6,8},{7,5},{8,10},{9,7},{10,... | collective-permute-start | bytes 1419272 | tf_op jit(solution)/shard_map/ppermute | solution.py:191
  75.9 0.0 collective-permute-done.7.refs_5_
  75.9 5.0 %collective-permute-start.8 = (bf16[264,896]{1,0:T(8,128)(2,1)S(1)}, bf16[264,896]{1,0:T(8,128)(2,1)}, u32[]{:S(2)}, u32[]{:S(2)}) collective-permute-start(bf16[264,896]{1,0:T(8,128)(2,1)S(1)} %collective-permute-done.7.refs_5_), channel_id=1, source_target_pairs={{0,2},{1,15},{2,4},{3,1},{4,6},{5,3},{6,8},{7,5},{8,10},{9,7},{10,... | collective-permute-start | bytes 1419272 | tf_op jit(solution)/shard_map/ppermute | solution.py:193
  80.9 0.0 copy-start.1
  80.9 0.8 copy-done.1
  81.7 0.0 collective-permute-done.3.refs_2_
  81.7 4.7 %collective-permute-start.4 = (bf16[264,896]{1,0:T(8,128)(2,1)S(1)}, bf16[264,896]{1,0:T(8,128)(2,1)}, u32[]{:S(2)}, u32[]{:S(2)}) collective-permute-start(bf16[264,896]{1,0:T(8,128)(2,1)S(1)} %collective-permute-done.3.refs_2_), channel_id=1, source_target_pairs={{0,2},{1,15},{2,4},{3,1},{4,6},{5,3},{6,8},{7,5},{8,10},{9,7},{10,... | collective-permute-start | bytes 1419272 | tf_op jit(solution)/shard_map/ppermute | solution.py:191
  86.4 0.0 copy-start.3
  86.5 0.8 copy-done.3
  87.2 0.0 collective-permute-done.8.refs_6_
  87.2 4.4 %collective-permute-start.9 = (bf16[264,896]{1,0:T(8,128)(2,1)}, bf16[264,896]{1,0:T(8,128)(2,1)S(1)}, u32[]{:S(2)}, u32[]{:S(2)}) collective-permute-start(bf16[264,896]{1,0:T(8,128)(2,1)} %collective-permute-done.8.refs_6_), channel_id=1, source_target_pairs={{0,2},{1,15},{2,4},{3,1},{4,6},{5,3},{6,8},{7,5},{8,10},{9,7},{10,... | collective-permute-start | bytes 1419272 | tf_op jit(solution)/shard_map/ppermute | solution.py:193
  91.6 0.4 collective-permute-done.4.refs_3_
  92.0 5.1 %collective-permute-start.5 = (bf16[264,896]{1,0:T(8,128)(2,1)}, bf16[264,896]{1,0:T(8,128)(2,1)}, u32[]{:S(2)}, u32[]{:S(2)}) collective-permute-start(bf16[264,896]{1,0:T(8,128)(2,1)} %collective-permute-done.4.refs_3_), channel_id=1, source_target_pairs={{0,2},{1,15},{2,4},{3,1},{4,6},{5,3},{6,8},{7,5},{8,10},{9,7},{10,... | collective-permute-start | bytes 1419272 | tf_op jit(solution)/shard_map/ppermute | solution.py:191
  97.2 0.1 concatenate.3.place_ref
  97.3 0.2 collective-permute-done.9.shard_ref.refs_7_
  97.5 5.5 %collective-permute-done.5.refs_4_ = bf16[264,896]{1,0:T(8,128)(2,1)} collective-permute-done((bf16[264,896]{1,0:T(8,128)(2,1)}, bf16[264,896]{1,0:T(8,128)(2,1)}, u32[]{:S(2)}, u32[]{:S(2)}) %collective-permute-start.5) | collective-permute-done | bytes 473120 | tf_op jit(solution)/shard_map/ppermute | solution.py:191
  103.0 0.0 copy-start
  103.0 1.5 %copy-done = bf16[128,7168]{1,0:T(8,128)(2,1)S(1)} copy-done((bf16[128,7168]{1,0:T(8,128)(2,1)S(1)}, bf16[128,7168]{1,0:T(8,128)(2,1)}, u32[]{:S(2)}) %copy-start) | copy-done | bytes 1835032
  104.5 0.0 copy-start.2
  104.5 1.0 copy-done.2
  105.5 0.0 copy-start.4
  105.5 1.0 copy-done.4
  106.5 0.0 copy-start.6
  106.5 0.9 copy-done.6
  107.5 3.7 %shard_map.71 = (bf16[512,128]{1,0:T(8,128)(2,1)S(1)}, bf16[256,128]{1,0:T(8,128)(2,1)S(1)}, f32[16,1,128]{2,1,0:T(1,128)}) custom-call(s32[9]{0:T(128)S(1)} %concatenate.3.place_ref, bf16[264,896]{1,0:T(8,128)(2,1)S(1)} %shard_map.69.refs_0_, bf16[264,896]{1,0:T(8,128)(2,1)S(1)} %collective-permute-done.2.refs_1_, bf16[264,896]{1,0:T(8,128)(2,1)S(1)} %copy-done.4, ...), custom_call_target="tpu_custom_call" | custom-call | tf_op jit(solution)/shard_map/pallas_call | solution.py:143
  111.1 0.0 copy-start.7
  111.1 0.6 copy-done.7
  111.8 11.9 %all-to-all-start.1 = ((f32[16,1,128]{2,1,0:T(1,128)}), f32[16,1,128]{2,1,0:T(1,128)S(1)}, u32[]{:S(2)}, u32[]{:S(2)}) async-start(f32[16,1,128]{2,1,0:T(1,128)} %get-tuple-element.7), calls=%async_computation.1 | async-start | bytes 16384 | tf_op jit(solution)/shard_map/all_to_all | solution.py:222
  123.7 2.0 %collective-permute-start.10 = (bf16[256,128]{1,0:T(8,128)(2,1)S(1)}, bf16[256,128]{1,0:T(8,128)(2,1)S(1)}, u32[]{:S(2)}, u32[]{:S(2)}) collective-permute-start(bf16[256,128]{1,0:T(8,128)(2,1)S(1)} %get-tuple-element.6), channel_id=1, source_target_pairs={{0,1},{1,0},{2,3},{3,2},{4,5},{5,4},{6,7},{7,6},{8,9},{9,8},{10,11... | collective-permute-start | bytes 196616 | tf_op jit(solution)/shard_map/ppermute | solution.py:221
  125.7 4.9 %all-to-all-done.1 = f32[16,1,128]{2,1,0:T(1,128)S(1)} async-done(((f32[16,1,128]{2,1,0:T(1,128)}), f32[16,1,128]{2,1,0:T(1,128)S(1)}, u32[]{:S(2)}, u32[]{:S(2)}) %all-to-all-start.1) | async-done | bytes 8224 | tf_op jit(solution)/shard_map/all_to_all | solution.py:222
  130.6 0.1 reshape.32
  130.7 0.6 broadcast_in_dim.12
  131.3 6.1 %all-to-all-start.2 = ((f32[64,1,128]{2,1,0:T(1,128)}), f32[64,1,128]{2,1,0:T(1,128)S(1)}, u32[]{:S(2)}, u32[]{:S(2)}) async-start(f32[64,1,128]{2,1,0:T(1,128)} %broadcast_in_dim.12), calls=%async_computation.2 | async-start | bytes 65536 | tf_op jit(solution)/shard_map/all_to_all | solution.py:225
  137.6 0.1 copy.11
  137.7 0.1 tile.7
  137.8 0.1 eq.34
  137.8 0.1 stack.59.place_ref
  137.9 0.0 collective-permute-done.10.got_ref
  137.9 1.6 %shard_map.72 = bf16[512,128]{1,0:T(8,128)(2,1)} custom-call(s32[8]{0:T(128)S(1)} %stack.59.place_ref, bf16[512,128]{1,0:T(8,128)(2,1)} %copy-done.7, bf16[256,128]{1,0:T(8,128)(2,1)S(1)} %collective-permute-done.10.got_ref), custom_call_target="tpu_custom_call" | custom-call | tf_op jit(solution)/shard_map/pallas_call | solution.py:143
  139.5 8.8 %all-to-all-done.2 = f32[64,1,128]{2,1,0:T(1,128)S(1)} async-done(((f32[64,1,128]{2,1,0:T(1,128)}), f32[64,1,128]{2,1,0:T(1,128)S(1)}, u32[]{:S(2)}, u32[]{:S(2)}) %all-to-all-start.2) | async-done | bytes 32800 | tf_op jit(solution)/shard_map/all_to_all | solution.py:225
  148.3 0.1 reshape.33
  148.4 0.7 copy.12
  (5 shorter events, 0.1 us)
Async XLA Ops:
  0.6 54.2 %copy-start.8 = (s32[8,4]{0,1:T(4,128)S(1)}, s32[8,4]{0,1:T(4,128)}, u32[]{:S(2)}) copy-start(s32[8,4]{0,1:T(4,128)} %param.7) | copy-start | bytes 388
  0.6 29.7 %copy-start.5 = (bf16[1,512,128]{2,1,0:T(8,128)(2,1)S(1)}, bf16[1,512,128]{2,1,0:T(8,128)(2,1)}, u32[]{:S(2)}) copy-start(bf16[1,512,128]{2,1,0:T(8,128)(2,1)} %param.8) | copy-start | bytes 393220
  3.5 51.4 %all-to-all-start = ((bf16[64,8,1024]{2,1,0:T(8,128)(2,1)}), bf16[64,8,1024]{2,1,0:T(8,128)(2,1)S(1)}, u32[]{:S(2)}, u32[]{:S(2)}) async-start(bf16[64,8,1024]{2,1,0:T(8,128)(2,1)} %bitcast.20), calls=%async_computation | async-start | bytes 2097152 | tf_op jit(solution)/shard_map/all_to_all | solution.py:174
  27.4 6.5 %collective-permute-start = (bf16[128,7168]{1,0:T(8,128)(2,1)}, bf16[128,7168]{1,0:T(8,128)(2,1)S(1)}, u32[]{:S(2)}, u32[]{:S(2)}) collective-permute-start(bf16[128,7168]{1,0:T(8,128)(2,1)} %refs_9_.1), channel_id=1, source_target_pairs={{0,1},{1,0},{2,3},{3,2},{4,5},{5,4},{6,7},{7,6},{8,9},{9,8},{10,11... | collective-permute-start | bytes 5505032 | tf_op jit(solution)/shard_map/ppermute | solution.py:177
  30.3 3.6 %collective-permute-start.1 = (bf16[512,128]{1,0:T(8,128)(2,1)S(1)}, bf16[512,128]{1,0:T(8,128)(2,1)S(1)}, u32[]{:S(2)}, u32[]{:S(2)}) collective-permute-start(bf16[512,128]{1,0:T(8,128)(2,1)S(1)} %bitcast.31), channel_id=1, source_target_pairs={{0,1},{1,0},{2,3},{3,2},{4,5},{5,4},{6,7},{7,6},{8,9},{9,8},{10,11... | collective-permute-start | bytes 393224 | tf_op jit(solution)/shard_map/ppermute | solution.py:178
  55.6 9.7 %collective-permute-start.6 = (bf16[264,896]{1,0:T(8,128)(2,1)S(1)}, bf16[264,896]{1,0:T(8,128)(2,1)S(1)}, u32[]{:S(2)}, u32[]{:S(2)}) collective-permute-start(bf16[264,896]{1,0:T(8,128)(2,1)S(1)} %shard_map.69.refs_0_), channel_id=1, source_target_pairs={{0,1},{1,0},{2,3},{3,2},{4,5},{5,4},{6,7},{7,6},{8,9},{9,8},{10,11... | collective-permute-start | bytes 1419272 | tf_op jit(solution)/shard_map/ppermute | solution.py:189
  60.8 10.1 %collective-permute-start.2 = (bf16[264,896]{1,0:T(8,128)(2,1)S(1)}, bf16[264,896]{1,0:T(8,128)(2,1)S(1)}, u32[]{:S(2)}, u32[]{:S(2)}) collective-permute-start(bf16[264,896]{1,0:T(8,128)(2,1)S(1)} %shard_map.69.refs_0_), channel_id=1, source_target_pairs={{0,2},{1,15},{2,4},{3,1},{4,6},{5,3},{6,8},{7,5},{8,10},{9,7},{10,... | collective-permute-start | bytes 1419272 | tf_op jit(solution)/shard_map/ppermute | solution.py:191
  65.3 10.6 %collective-permute-start.7 = (bf16[264,896]{1,0:T(8,128)(2,1)S(1)}, bf16[264,896]{1,0:T(8,128)(2,1)S(1)}, u32[]{:S(2)}, u32[]{:S(2)}) collective-permute-start(bf16[264,896]{1,0:T(8,128)(2,1)S(1)} %collective-permute-done.6), channel_id=1, source_target_pairs={{0,2},{1,15},{2,4},{3,1},{4,6},{5,3},{6,8},{7,5},{8,10},{9,7},{10,... | collective-permute-start | bytes 1419272 | tf_op jit(solution)/shard_map/ppermute | solution.py:193
  70.8 10.9 %collective-permute-start.3 = (bf16[264,896]{1,0:T(8,128)(2,1)S(1)}, bf16[264,896]{1,0:T(8,128)(2,1)S(1)}, u32[]{:S(2)}, u32[]{:S(2)}) collective-permute-start(bf16[264,896]{1,0:T(8,128)(2,1)S(1)} %collective-permute-done.2.refs_1_), channel_id=1, source_target_pairs={{0,2},{1,15},{2,4},{3,1},{4,6},{5,3},{6,8},{7,5},{8,10},{9,7},{10,... | collective-permute-start | bytes 1419272 | tf_op jit(solution)/shard_map/ppermute | solution.py:191
  75.9 11.3 %collective-permute-start.8 = (bf16[264,896]{1,0:T(8,128)(2,1)S(1)}, bf16[264,896]{1,0:T(8,128)(2,1)}, u32[]{:S(2)}, u32[]{:S(2)}) collective-permute-start(bf16[264,896]{1,0:T(8,128)(2,1)S(1)} %collective-permute-done.7.refs_5_), channel_id=1, source_target_pairs={{0,2},{1,15},{2,4},{3,1},{4,6},{5,3},{6,8},{7,5},{8,10},{9,7},{10,... | collective-permute-start | bytes 1419272 | tf_op jit(solution)/shard_map/ppermute | solution.py:193
  80.9 0.8 copy-start.1
  81.7 10.3 %collective-permute-start.4 = (bf16[264,896]{1,0:T(8,128)(2,1)S(1)}, bf16[264,896]{1,0:T(8,128)(2,1)}, u32[]{:S(2)}, u32[]{:S(2)}) collective-permute-start(bf16[264,896]{1,0:T(8,128)(2,1)S(1)} %collective-permute-done.3.refs_2_), channel_id=1, source_target_pairs={{0,2},{1,15},{2,4},{3,1},{4,6},{5,3},{6,8},{7,5},{8,10},{9,7},{10,... | collective-permute-start | bytes 1419272 | tf_op jit(solution)/shard_map/ppermute | solution.py:191
  86.4 0.8 copy-start.3
  87.2 10.3 %collective-permute-start.9 = (bf16[264,896]{1,0:T(8,128)(2,1)}, bf16[264,896]{1,0:T(8,128)(2,1)S(1)}, u32[]{:S(2)}, u32[]{:S(2)}) collective-permute-start(bf16[264,896]{1,0:T(8,128)(2,1)} %collective-permute-done.8.refs_6_), channel_id=1, source_target_pairs={{0,2},{1,15},{2,4},{3,1},{4,6},{5,3},{6,8},{7,5},{8,10},{9,7},{10,... | collective-permute-start | bytes 1419272 | tf_op jit(solution)/shard_map/ppermute | solution.py:193
  92.0 11.0 %collective-permute-start.5 = (bf16[264,896]{1,0:T(8,128)(2,1)}, bf16[264,896]{1,0:T(8,128)(2,1)}, u32[]{:S(2)}, u32[]{:S(2)}) collective-permute-start(bf16[264,896]{1,0:T(8,128)(2,1)} %collective-permute-done.4.refs_3_), channel_id=1, source_target_pairs={{0,2},{1,15},{2,4},{3,1},{4,6},{5,3},{6,8},{7,5},{8,10},{9,7},{10,... | collective-permute-start | bytes 1419272 | tf_op jit(solution)/shard_map/ppermute | solution.py:191
  103.0 1.5 %copy-start = (bf16[128,7168]{1,0:T(8,128)(2,1)S(1)}, bf16[128,7168]{1,0:T(8,128)(2,1)}, u32[]{:S(2)}) copy-start(bf16[128,7168]{1,0:T(8,128)(2,1)} %refs_9_.1) | copy-start | bytes 5505028
  104.5 1.0 copy-start.2
  105.5 1.0 copy-start.4
  106.5 0.9 copy-start.6
  111.1 0.6 copy-start.7
  111.8 18.8 %all-to-all-start.1 = ((f32[16,1,128]{2,1,0:T(1,128)}), f32[16,1,128]{2,1,0:T(1,128)S(1)}, u32[]{:S(2)}, u32[]{:S(2)}) async-start(f32[16,1,128]{2,1,0:T(1,128)} %get-tuple-element.7), calls=%async_computation.1 | async-start | bytes 16384 | tf_op jit(solution)/shard_map/all_to_all | solution.py:222
  123.7 14.3 %collective-permute-start.10 = (bf16[256,128]{1,0:T(8,128)(2,1)S(1)}, bf16[256,128]{1,0:T(8,128)(2,1)S(1)}, u32[]{:S(2)}, u32[]{:S(2)}) collective-permute-start(bf16[256,128]{1,0:T(8,128)(2,1)S(1)} %get-tuple-element.6), channel_id=1, source_target_pairs={{0,1},{1,0},{2,3},{3,2},{4,5},{5,4},{6,7},{7,6},{8,9},{9,8},{10,11... | collective-permute-start | bytes 196616 | tf_op jit(solution)/shard_map/ppermute | solution.py:221
  131.3 17.0 %all-to-all-start.2 = ((f32[64,1,128]{2,1,0:T(1,128)}), f32[64,1,128]{2,1,0:T(1,128)S(1)}, u32[]{:S(2)}, u32[]{:S(2)}) async-start(f32[64,1,128]{2,1,0:T(1,128)} %broadcast_in_dim.12), calls=%async_computation.2 | async-start | bytes 65536 | tf_op jit(solution)/shard_map/all_to_all | solution.py:225

commit v3 on v2

--- a/solution.py
+++ b/solution.py
@@ -70,29 +70,32 @@
     out_ref[rows:, :] = jnp.concatenate([prob, pad], axis=1).astype(BF)
 
 
-def terms_kernel(place_ref, *refs):
-    shards, last_prob = refs[:-8], refs[-8]
-    own_w, mate_w, own_gate, mate_gate, pre_ref, give_ref, sum_ref = refs[-7:]
-    count = len(shards)
+def multiply(shards, own_w, mate_w):
     rows = (shards[0].shape[0] - SUB) // SUB
     width, model = own_w.shape
     wide = model // SUB
-    hidden = jnp.zeros((count * rows, 2 * width), F32)
+    hidden = jnp.zeros((len(shards) * rows, 2 * width), F32)
     for e in range(SUB):
         left = jnp.concatenate([ref[e * rows : (e + 1) * rows, :] for ref in shards], axis=0)
         cols = slice(e * wide, (e + 1) * wide)
         right = jnp.concatenate([own_w[:, cols], mate_w[:, cols]], axis=0)
         hidden += lax.dot_general(left, right, NT, preferred_element_type=F32)
-    expert = jnp.where(iota((SUB, width), 0) == place_ref[count], 1.0, 0.0).astype(BF)
+    return hidden
+
+
+def finish(place_ref, first, shards, hidden, gates, pre_ref, give_ref, sum_ref):
+    rows = (shards[0].shape[0] - SUB) // SUB
+    width = gates[0].shape[1]
+    mine = place_ref[place_ref.shape[0] - 1]
+    expert = jnp.where(iota((SUB, width), 0) == mine, 1.0, 0.0).astype(BF)
     terms = []
     for i, ref in enumerate(shards):
-        at = pl.ds(pl.multiple_of(place_ref[i] * rows, rows), rows)
-        prob = last_prob[...] if i == count - 1 else ref[SUB * rows :, :]
+        at = pl.ds(pl.multiple_of(place_ref[first + i] * rows, rows), rows)
         scale = lax.dot_general(
-            prob[:, :rows], expert, TN, preferred_element_type=F32
+            ref[SUB * rows :, :rows], expert, TN, preferred_element_type=F32
         )
         total = jnp.zeros((rows, width), F32)
-        for half, gate in enumerate((own_gate, mate_gate)):
+        for half, gate in enumerate(gates):
             grad = hidden[i * rows : (i + 1) * rows, half * width : (half + 1) * width]
             value = gate[at, :].astype(F32)
             sigma = jax.nn.sigmoid(value)
@@ -102,7 +105,7 @@
             if half == 0:
                 pre_ref[at, :] = result
             else:
-                give_ref[i * rows : (i + 1) * rows, :] = result
+                give_ref[(first + i) * rows : (first + i + 1) * rows, :] = result
         terms.append(total)
     sums = lax.dot_general(
         jnp.ones((SUB, width), F32),
@@ -111,13 +114,26 @@
         precision=lax.Precision.HIGHEST,
         preferred_element_type=F32,
     )
+    for i in range(len(shards)):
+        sum_ref[pl.ds(place_ref[first + i], 1), 0, :rows] = sums[:1, i * rows : (i + 1) * rows]
+
+
+def early_kernel(place_ref, *refs):
+    shards, (own_w, mate_w, own_gate, mate_gate, pre_ref, give_ref, sum_ref) = refs[:-7], refs[-7:]
+    hidden = multiply(shards, own_w, mate_w)
+    pre_ref[...] = jnp.zeros(pre_ref.shape, BF)
+    give_ref[...] = jnp.zeros(give_ref.shape, BF)
     sum_ref[...] = jnp.zeros(sum_ref.shape, F32)
-    for i in range(count):
-        sum_ref[pl.ds(place_ref[i], 1), 0, :rows] = sums[:1, i * rows : (i + 1) * rows]
-
-
-def prob_kernel(shard_ref, out_ref):
-    out_ref[...] = shard_ref[shard_ref.shape[0] - SUB :, :]
+    gates = (own_gate, mate_gate)
+    finish(place_ref, 0, shards, hidden, gates, pre_ref, give_ref, sum_ref)
+
+
+def last_kernel(place_ref, shard, own_w, mate_w, own_gate, mate_gate, *refs):
+    ins, outs = refs[:3], refs[3:]
+    hidden = multiply([shard], own_w, mate_w)
+    for source, target in zip(ins, outs):
+        target[...] = source[...]
+    finish(place_ref, place_ref.shape[0] - 2, [shard], hidden, (own_gate, mate_gate), *outs)
 
 
 def join_kernel(place_ref, half_ref, got_ref, out_ref):
@@ -191,32 +207,29 @@
         near.append(move(near[-1], perm=ahead))
         if step < chips // 2 - 1:
             far.append(move(far[-1], perm=ahead))
-    shards = near + far[1:]
+    shards = near[:-1] + far[1:] + near[-1:]
     count = len(shards)
 
     def places(at):
         chip, core = at // 2, at % 2
         step = 2 * core - 1
-        hops = [(k, core) for k in range(chips // 2 + 1)] + [(k, 1 - core) for k in range(1, chips // 2)]
+        last = chips // 2
+        hops = [(k, core) for k in range(last)] + [(k, 1 - core) for k in range(1, last)]
+        hops.append((last, core))
         return jnp.stack([(chip + step * k) % chips * 2 + c for k, c in hops]).astype(jnp.int32)
 
     place = jnp.concatenate([places(loc), (loc // (locs // experts)).reshape(1)])
-    last_prob = call(prob_kernel, [VMEM], shape((SUB, wide), BF), far[-1])
+    results = [
+        shape(gate_rows.shape, BF),
+        shape((count * rows, width), BF),
+        shape((locs, 1, LANES), F32),
+    ]
+    shared = (down_weight, mate_w, gate_rows, mate_gate)
+    early = call(
+        early_kernel, [SMEM] + [VMEM] * (count + 3), results, place, *shards[:-1], *shared
+    )
     half, give, sums = call(
-        terms_kernel,
-        [SMEM] + [VMEM] * (count + 5),
-        [
-            shape(gate_rows.shape, BF),
-            shape((count * rows, width), BF),
-            shape((locs, 1, LANES), F32),
-        ],
-        place,
-        *shards,
-        last_prob,
-        down_weight,
-        mate_w,
-        gate_rows,
-        mate_gate,
+        last_kernel, [SMEM] + [VMEM] * 8, results, place, shards[-1], *shared, *early
     )
     got = move(give, perm=swap)
     parts = lax.all_to_all(sums, "loc", split_axis=0, concat_axis=0, tiled=True)

time: 150 us -> 145 us (0.967)
  waiting for transfers between devices: 44.9 us -> 39.4 us
  Pallas kernels: 8.76 us -> 10.8 us
    ppermute x4, waiting for transfers between devices: 8.37 us -> 2.9 us  [body(): near.append(move(near[-1], perm=ahead))]
    pallas_call x5, Pallas kernels: 8.76 us -> 10.8 us  [call(): pl.pallas_call(kernel, in_specs=specs, out_shape=shapes, compiler_params=...]
  transfers between devices with their start and end apart: 14 -> 14, of which waited for: 8 -> 7; matrix products, arithmetic and copies ran while one was open for 1% -> 1% of each run, Pallas kernels for 1% -> 3%
where the time goes in v3:
time: 145 us
  starting transfers between devices  84.6 us (58%)
  waiting for transfers between devices  39.4 us (27%)
  Pallas kernels  10.8 us (7%)
  local copies, waits for them, and re-layouts  8.59 us (6%)
    all_to_all x1, starting transfers between devices, body(): lax.all_to_all(send.reshape(groups, SUB, -1), 'grp', split_axis=0, concat...  24 us
    all_to_all x1, waiting for transfers between devices, body(): lax.all_to_all(send.reshape(groups, SUB, -1), 'grp', split_axis=0, concat...  21 us
    ppermute x4, starting transfers between devices, body(): near.append(move(near[-1], perm=ahead))  19.3 us
    ppermute x3, starting transfers between devices, body(): far.append(move(far[-1], perm=ahead))  12.4 us
    pallas_call x5, Pallas kernels, call(): pl.pallas_call(kernel, in_specs=specs, out_shape=shapes, compiler_params=...  10.8 us
    all_to_all x1, starting transfers between devices, body(): parts = lax.all_to_all(sums, 'loc', split_axis=0, concat_axis=0, tiled=True)  10.7 us
    all_to_all x1, waiting for transfers between devices, body(): lax.all_to_all(jnp.broadcast_to(lane, (groups, 1, LANES)), 'grp', split_a...  8.77 us
    unnamed x20, local copies, waits for them, and re-layouts  7.45 us
  transfers between devices with their start and end apart: 14, of which 7 were waited for; matrix products, arithmetic and copies ran while one was open for 1% of the time, Pallas kernels for 3%

profile of v3, /device:TPU:1, one launch (start us, length us, event | category | flops | bytes accessed | tf_op | source)
XLA Modules:
  0.0 144.6 jit_solution(1420005797397159202)
XLA Ops:
  0.6 0.0 copy-start.8
  0.6 0.0 copy-start.1
  0.7 2.8 %shard_map.68 = bf16[512,1024]{1,0:T(8,128)(2,1)} custom-call(bf16[8,7168]{1,0:T(8,128)(2,1)} %grad_ref.1, s32[4,8]{1,0:T(4,128)} %bitcast.34, bf16[4,2,8]{2,1,0:T(2,128)(2,1)} %bitcast.40), custom_call_target="tpu_custom_call" | custom-call | tf_op jit(solution)/shard_map/pallas_call | solution.py:159
  3.5 24.0 %all-to-all-start = ((bf16[64,8,1024]{2,1,0:T(8,128)(2,1)}), bf16[64,8,1024]{2,1,0:T(8,128)(2,1)S(1)}, u32[]{:S(2)}, u32[]{:S(2)}) async-start(bf16[64,8,1024]{2,1,0:T(8,128)(2,1)} %bitcast.20), calls=%async_computation | async-start | bytes 2097152 | tf_op jit(solution)/shard_map/all_to_all | solution.py:190
  27.4 2.9 %collective-permute-start = (bf16[128,7168]{1,0:T(8,128)(2,1)}, bf16[128,7168]{1,0:T(8,128)(2,1)S(1)}, u32[]{:S(2)}, u32[]{:S(2)}) collective-permute-start(bf16[128,7168]{1,0:T(8,128)(2,1)} %own_w.1), channel_id=1, source_target_pairs={{0,1},{1,0},{2,3},{3,2},{4,5},{5,4},{6,7},{7,6},{8,9},{9,8},{10,11... | collective-permute-start | bytes 5505032 | tf_op jit(solution)/shard_map/ppermute | solution.py:193
  30.3 0.0 copy-done.1
  30.3 1.9 %collective-permute-start.1 = (bf16[512,128]{1,0:T(8,128)(2,1)S(1)}, bf16[512,128]{1,0:T(8,128)(2,1)S(1)}, u32[]{:S(2)}, u32[]{:S(2)}) collective-permute-start(bf16[512,128]{1,0:T(8,128)(2,1)S(1)} %bitcast.31), channel_id=1, source_target_pairs={{0,1},{1,0},{2,3},{3,2},{4,5},{5,4},{6,7},{7,6},{8,9},{9,8},{10,11... | collective-permute-start | bytes 393224 | tf_op jit(solution)/shard_map/ppermute | solution.py:194
  32.2 1.6 %collective-permute-done.1.refs_1_.refs_10_.mate_gate = bf16[512,128]{1,0:T(8,128)(2,1)S(1)} collective-permute-done((bf16[512,128]{1,0:T(8,128)(2,1)S(1)}, bf16[512,128]{1,0:T(8,128)(2,1)S(1)}, u32[]{:S(2)}, u32[]{:S(2)}) %collective-permute-start.1) | collective-permute-done | bytes 131104 | tf_op jit(solution)/shard_map/ppermute | solution.py:194
  33.9 0.0 collective-permute-done.refs_0_.refs_8_.mate_w
  33.9 21.0 %all-to-all-done = bf16[64,8,1024]{2,1,0:T(8,128)(2,1)S(1)} async-done(((bf16[64,8,1024]{2,1,0:T(8,128)(2,1)}), bf16[64,8,1024]{2,1,0:T(8,128)(2,1)S(1)}, u32[]{:S(2)}, u32[]{:S(2)}) %all-to-all-start) | async-done | bytes 1048608 | tf_op jit(solution)/shard_map/all_to_all | solution.py:190
  54.9 0.0 copy-done.8
  54.9 0.7 shard_map.69.refs_0_
  55.6 5.2 %collective-permute-start.6 = (bf16[264,896]{1,0:T(8,128)(2,1)S(1)}, bf16[264,896]{1,0:T(8,128)(2,1)S(1)}, u32[]{:S(2)}, u32[]{:S(2)}) collective-permute-start(bf16[264,896]{1,0:T(8,128)(2,1)S(1)} %shard_map.69.refs_0_), channel_id=1, source_target_pairs={{0,1},{1,0},{2,3},{3,2},{4,5},{5,4},{6,7},{7,6},{8,9},{9,8},{10,11... | collective-permute-start | bytes 1419272 | tf_op jit(solution)/shard_map/ppermute | solution.py:205
  60.8 4.5 %collective-permute-start.2 = (bf16[264,896]{1,0:T(8,128)(2,1)S(1)}, bf16[264,896]{1,0:T(8,128)(2,1)S(1)}, u32[]{:S(2)}, u32[]{:S(2)}) collective-permute-start(bf16[264,896]{1,0:T(8,128)(2,1)S(1)} %shard_map.69.refs_0_), channel_id=1, source_target_pairs={{0,2},{1,15},{2,4},{3,1},{4,6},{5,3},{6,8},{7,5},{8,10},{9,7},{10,... | collective-permute-start | bytes 1419272 | tf_op jit(solution)/shard_map/ppermute | solution.py:207
  65.3 0.0 collective-permute-done.6
  65.3 3.1 %collective-permute-start.7 = (bf16[264,896]{1,0:T(8,128)(2,1)S(1)}, bf16[264,896]{1,0:T(8,128)(2,1)S(1)}, u32[]{:S(2)}, u32[]{:S(2)}) collective-permute-start(bf16[264,896]{1,0:T(8,128)(2,1)S(1)} %collective-permute-done.6), channel_id=1, source_target_pairs={{0,2},{1,15},{2,4},{3,1},{4,6},{5,3},{6,8},{7,5},{8,10},{9,7},{10,... | collective-permute-start | bytes 1419272 | tf_op jit(solution)/shard_map/ppermute | solution.py:209
  68.4 2.5 %collective-permute-done.2.refs_1_ = bf16[264,896]{1,0:T(8,128)(2,1)S(1)} collective-permute-done((bf16[264,896]{1,0:T(8,128)(2,1)S(1)}, bf16[264,896]{1,0:T(8,128)(2,1)S(1)}, u32[]{:S(2)}, u32[]{:S(2)}) %collective-permute-start.2) | collective-permute-done | bytes 473120 | tf_op jit(solution)/shard_map/ppermute | solution.py:207
  70.9 5.0 %collective-permute-start.3 = (bf16[264,896]{1,0:T(8,128)(2,1)S(1)}, bf16[264,896]{1,0:T(8,128)(2,1)S(1)}, u32[]{:S(2)}, u32[]{:S(2)}) collective-permute-start(bf16[264,896]{1,0:T(8,128)(2,1)S(1)} %collective-permute-done.2.refs_1_), channel_id=1, source_target_pairs={{0,2},{1,15},{2,4},{3,1},{4,6},{5,3},{6,8},{7,5},{8,10},{9,7},{10,... | collective-permute-start | bytes 1419272 | tf_op jit(solution)/shard_map/ppermute | solution.py:207
  75.9 0.0 collective-permute-done.7.refs_4_
  75.9 5.0 %collective-permute-start.8 = (bf16[264,896]{1,0:T(8,128)(2,1)S(1)}, bf16[264,896]{1,0:T(8,128)(2,1)}, u32[]{:S(2)}, u32[]{:S(2)}) collective-permute-start(bf16[264,896]{1,0:T(8,128)(2,1)S(1)} %collective-permute-done.7.refs_4_), channel_id=1, source_target_pairs={{0,2},{1,15},{2,4},{3,1},{4,6},{5,3},{6,8},{7,5},{8,10},{9,7},{10,... | collective-permute-start | bytes 1419272 | tf_op jit(solution)/shard_map/ppermute | solution.py:209
  81.0 0.0 copy-start.3
  81.0 0.8 copy-done.3
  81.8 0.0 collective-permute-done.3.refs_2_
  81.8 4.7 %collective-permute-start.4 = (bf16[264,896]{1,0:T(8,128)(2,1)S(1)}, bf16[264,896]{1,0:T(8,128)(2,1)}, u32[]{:S(2)}, u32[]{:S(2)}) collective-permute-start(bf16[264,896]{1,0:T(8,128)(2,1)S(1)} %collective-permute-done.3.refs_2_), channel_id=1, source_target_pairs={{0,2},{1,15},{2,4},{3,1},{4,6},{5,3},{6,8},{7,5},{8,10},{9,7},{10,... | collective-permute-start | bytes 1419272 | tf_op jit(solution)/shard_map/ppermute | solution.py:207
  86.5 0.0 copy-start.5
  86.5 0.8 copy-done.5
  87.2 0.0 collective-permute-done.8.refs_5_
  87.2 4.4 %collective-permute-start.9 = (bf16[264,896]{1,0:T(8,128)(2,1)}, bf16[264,896]{1,0:T(8,128)(2,1)}, u32[]{:S(2)}, u32[]{:S(2)}) collective-permute-start(bf16[264,896]{1,0:T(8,128)(2,1)} %collective-permute-done.8.refs_5_), channel_id=1, source_target_pairs={{0,2},{1,15},{2,4},{3,1},{4,6},{5,3},{6,8},{7,5},{8,10},{9,7},{10,... | collective-permute-start | bytes 1419272 | tf_op jit(solution)/shard_map/ppermute | solution.py:209
  91.6 0.4 collective-permute-done.4.refs_3_
  92.0 5.1 %collective-permute-start.5 = (bf16[264,896]{1,0:T(8,128)(2,1)}, bf16[264,896]{1,0:T(8,128)(2,1)S(1)}, u32[]{:S(2)}, u32[]{:S(2)}) collective-permute-start(bf16[264,896]{1,0:T(8,128)(2,1)} %collective-permute-done.4.refs_3_), channel_id=1, source_target_pairs={{0,2},{1,15},{2,4},{3,1},{4,6},{5,3},{6,8},{7,5},{8,10},{9,7},{10,... | collective-permute-start | bytes 1419272 | tf_op jit(solution)/shard_map/ppermute | solution.py:207
  97.3 0.1 concatenate.3.place_ref
  97.3 0.2 collective-permute-done.9.refs_6_
  97.5 0.0 copy-start
  97.5 1.5 %copy-done = bf16[128,7168]{1,0:T(8,128)(2,1)S(1)} copy-done((bf16[128,7168]{1,0:T(8,128)(2,1)S(1)}, bf16[128,7168]{1,0:T(8,128)(2,1)}, u32[]{:S(2)}) %copy-start) | copy-done | bytes 1835032
  99.0 0.0 copy-start.2
  99.0 0.9 copy-done.2
  99.9 0.0 copy-start.4
  99.9 1.0 copy-done.4
  100.9 0.0 copy-start.6
  100.9 1.0 copy-done.6
  102.0 3.2 %shard_map.70 = (bf16[512,128]{1,0:T(8,128)(2,1)S(1)}, bf16[256,128]{1,0:T(8,128)(2,1)S(1)}, f32[16,1,128]{2,1,0:T(1,128)S(1)}) custom-call(s32[9]{0:T(128)S(1)} %concatenate.3.place_ref, bf16[264,896]{1,0:T(8,128)(2,1)S(1)} %shard_map.69.refs_0_, bf16[264,896]{1,0:T(8,128)(2,1)S(1)} %collective-permute-done.2.refs_1_, bf16[264,896]{1,0:T(8,128)(2,1)S(1)} %copy-done.6, ...), custom_call_target="tpu_custom_call" | custom-call | tf_op jit(solution)/shard_map/pallas_call | solution.py:159
  105.2 0.0 collective-permute-done.5.shard
  105.3 2.5 %shard_map.71 = (bf16[512,128]{1,0:T(8,128)(2,1)S(1)}, bf16[256,128]{1,0:T(8,128)(2,1)S(1)}, f32[16,1,128]{2,1,0:T(1,128)}) custom-call(s32[9]{0:T(128)S(1)} %concatenate.3.place_ref, bf16[264,896]{1,0:T(8,128)(2,1)S(1)} %collective-permute-done.5.shard, bf16[128,7168]{1,0:T(8,128)(2,1)S(1)} %copy-done, ...), custom_call_target="tpu_custom_call" | custom-call | tf_op jit(solution)/shard_map/pallas_call | solution.py:159
  107.7 0.0 copy-start.7
  107.7 0.6 copy-done.7
  108.4 10.7 %all-to-all-start.1 = ((f32[16,1,128]{2,1,0:T(1,128)}), f32[16,1,128]{2,1,0:T(1,128)S(1)}, u32[]{:S(2)}, u32[]{:S(2)}) async-start(f32[16,1,128]{2,1,0:T(1,128)} %get-tuple-element.13), calls=%async_computation.1 | async-start | bytes 16384 | tf_op jit(solution)/shard_map/all_to_all | solution.py:235
  119.1 2.0 %collective-permute-start.10 = (bf16[256,128]{1,0:T(8,128)(2,1)S(1)}, bf16[256,128]{1,0:T(8,128)(2,1)S(1)}, u32[]{:S(2)}, u32[]{:S(2)}) collective-permute-start(bf16[256,128]{1,0:T(8,128)(2,1)S(1)} %get-tuple-element.12), channel_id=1, source_target_pairs={{0,1},{1,0},{2,3},{3,2},{4,5},{5,4},{6,7},{7,6},{8,9},{9,8},{10,11... | collective-permute-start | bytes 196616 | tf_op jit(solution)/shard_map/ppermute | solution.py:234
  121.1 4.9 %all-to-all-done.1 = f32[16,1,128]{2,1,0:T(1,128)S(1)} async-done(((f32[16,1,128]{2,1,0:T(1,128)}), f32[16,1,128]{2,1,0:T(1,128)S(1)}, u32[]{:S(2)}, u32[]{:S(2)}) %all-to-all-start.1) | async-done | bytes 8224 | tf_op jit(solution)/shard_map/all_to_all | solution.py:235
  126.1 0.1 reshape.32
  126.2 0.6 broadcast_in_dim.12
  126.8 6.1 %all-to-all-start.2 = ((f32[64,1,128]{2,1,0:T(1,128)}), f32[64,1,128]{2,1,0:T(1,128)S(1)}, u32[]{:S(2)}, u32[]{:S(2)}) async-start(f32[64,1,128]{2,1,0:T(1,128)} %broadcast_in_dim.12), calls=%async_computation.2 | async-start | bytes 65536 | tf_op jit(solution)/shard_map/all_to_all | solution.py:238
  133.1 0.1 copy.11
  133.1 0.1 tile.7
  133.2 0.1 eq.34
  133.3 0.1 stack.59.place_ref
  133.4 0.0 collective-permute-done.10.got_ref
  133.4 1.6 %shard_map.72 = bf16[512,128]{1,0:T(8,128)(2,1)} custom-call(s32[8]{0:T(128)S(1)} %stack.59.place_ref, bf16[512,128]{1,0:T(8,128)(2,1)} %copy-done.7, bf16[256,128]{1,0:T(8,128)(2,1)S(1)} %collective-permute-done.10.got_ref), custom_call_target="tpu_custom_call" | custom-call | tf_op jit(solution)/shard_map/pallas_call | solution.py:159
  135.0 8.8 %all-to-all-done.2 = f32[64,1,128]{2,1,0:T(1,128)S(1)} async-done(((f32[64,1,128]{2,1,0:T(1,128)}), f32[64,1,128]{2,1,0:T(1,128)S(1)}, u32[]{:S(2)}, u32[]{:S(2)}) %all-to-all-start.2) | async-done | bytes 32800 | tf_op jit(solution)/shard_map/all_to_all | solution.py:238
  143.8 0.1 reshape.33
  143.9 0.7 copy.12
  (4 shorter events, 0.1 us)
Async XLA Ops:
  0.6 54.2 %copy-start.8 = (s32[8,4]{0,1:T(4,128)S(1)}, s32[8,4]{0,1:T(4,128)}, u32[]{:S(2)}) copy-start(s32[8,4]{0,1:T(4,128)} %param.7) | copy-start | bytes 388
  0.6 29.7 %copy-start.1 = (bf16[1,512,128]{2,1,0:T(8,128)(2,1)S(1)}, bf16[1,512,128]{2,1,0:T(8,128)(2,1)}, u32[]{:S(2)}) copy-start(bf16[1,512,128]{2,1,0:T(8,128)(2,1)} %param.8) | copy-start | bytes 393220
  3.5 51.4 %all-to-all-start = ((bf16[64,8,1024]{2,1,0:T(8,128)(2,1)}), bf16[64,8,1024]{2,1,0:T(8,128)(2,1)S(1)}, u32[]{:S(2)}, u32[]{:S(2)}) async-start(bf16[64,8,1024]{2,1,0:T(8,128)(2,1)} %bitcast.20), calls=%async_computation | async-start | bytes 2097152 | tf_op jit(solution)/shard_map/all_to_all | solution.py:190
  27.4 6.5 %collective-permute-start = (bf16[128,7168]{1,0:T(8,128)(2,1)}, bf16[128,7168]{1,0:T(8,128)(2,1)S(1)}, u32[]{:S(2)}, u32[]{:S(2)}) collective-permute-start(bf16[128,7168]{1,0:T(8,128)(2,1)} %own_w.1), channel_id=1, source_target_pairs={{0,1},{1,0},{2,3},{3,2},{4,5},{5,4},{6,7},{7,6},{8,9},{9,8},{10,11... | collective-permute-start | bytes 5505032 | tf_op jit(solution)/shard_map/ppermute | solution.py:193
  30.3 3.6 %collective-permute-start.1 = (bf16[512,128]{1,0:T(8,128)(2,1)S(1)}, bf16[512,128]{1,0:T(8,128)(2,1)S(1)}, u32[]{:S(2)}, u32[]{:S(2)}) collective-permute-start(bf16[512,128]{1,0:T(8,128)(2,1)S(1)} %bitcast.31), channel_id=1, source_target_pairs={{0,1},{1,0},{2,3},{3,2},{4,5},{5,4},{6,7},{7,6},{8,9},{9,8},{10,11... | collective-permute-start | bytes 393224 | tf_op jit(solution)/shard_map/ppermute | solution.py:194
  55.6 9.7 %collective-permute-start.6 = (bf16[264,896]{1,0:T(8,128)(2,1)S(1)}, bf16[264,896]{1,0:T(8,128)(2,1)S(1)}, u32[]{:S(2)}, u32[]{:S(2)}) collective-permute-start(bf16[264,896]{1,0:T(8,128)(2,1)S(1)} %shard_map.69.refs_0_), channel_id=1, source_target_pairs={{0,1},{1,0},{2,3},{3,2},{4,5},{5,4},{6,7},{7,6},{8,9},{9,8},{10,11... | collective-permute-start | bytes 1419272 | tf_op jit(solution)/shard_map/ppermute | solution.py:205
  60.8 10.1 %collective-permute-start.2 = (bf16[264,896]{1,0:T(8,128)(2,1)S(1)}, bf16[264,896]{1,0:T(8,128)(2,1)S(1)}, u32[]{:S(2)}, u32[]{:S(2)}) collective-permute-start(bf16[264,896]{1,0:T(8,128)(2,1)S(1)} %shard_map.69.refs_0_), channel_id=1, source_target_pairs={{0,2},{1,15},{2,4},{3,1},{4,6},{5,3},{6,8},{7,5},{8,10},{9,7},{10,... | collective-permute-start | bytes 1419272 | tf_op jit(solution)/shard_map/ppermute | solution.py:207
  65.3 10.6 %collective-permute-start.7 = (bf16[264,896]{1,0:T(8,128)(2,1)S(1)}, bf16[264,896]{1,0:T(8,128)(2,1)S(1)}, u32[]{:S(2)}, u32[]{:S(2)}) collective-permute-start(bf16[264,896]{1,0:T(8,128)(2,1)S(1)} %collective-permute-done.6), channel_id=1, source_target_pairs={{0,2},{1,15},{2,4},{3,1},{4,6},{5,3},{6,8},{7,5},{8,10},{9,7},{10,... | collective-permute-start | bytes 1419272 | tf_op jit(solution)/shard_map/ppermute | solution.py:209
  70.9 10.9 %collective-permute-start.3 = (bf16[264,896]{1,0:T(8,128)(2,1)S(1)}, bf16[264,896]{1,0:T(8,128)(2,1)S(1)}, u32[]{:S(2)}, u32[]{:S(2)}) collective-permute-start(bf16[264,896]{1,0:T(8,128)(2,1)S(1)} %collective-permute-done.2.refs_1_), channel_id=1, source_target_pairs={{0,2},{1,15},{2,4},{3,1},{4,6},{5,3},{6,8},{7,5},{8,10},{9,7},{10,... | collective-permute-start | bytes 1419272 | tf_op jit(solution)/shard_map/ppermute | solution.py:207
  75.9 11.3 %collective-permute-start.8 = (bf16[264,896]{1,0:T(8,128)(2,1)S(1)}, bf16[264,896]{1,0:T(8,128)(2,1)}, u32[]{:S(2)}, u32[]{:S(2)}) collective-permute-start(bf16[264,896]{1,0:T(8,128)(2,1)S(1)} %collective-permute-done.7.refs_4_), channel_id=1, source_target_pairs={{0,2},{1,15},{2,4},{3,1},{4,6},{5,3},{6,8},{7,5},{8,10},{9,7},{10,... | collective-permute-start | bytes 1419272 | tf_op jit(solution)/shard_map/ppermute | solution.py:209
  81.0 0.8 copy-start.3
  81.8 10.3 %collective-permute-start.4 = (bf16[264,896]{1,0:T(8,128)(2,1)S(1)}, bf16[264,896]{1,0:T(8,128)(2,1)}, u32[]{:S(2)}, u32[]{:S(2)}) collective-permute-start(bf16[264,896]{1,0:T(8,128)(2,1)S(1)} %collective-permute-done.3.refs_2_), channel_id=1, source_target_pairs={{0,2},{1,15},{2,4},{3,1},{4,6},{5,3},{6,8},{7,5},{8,10},{9,7},{10,... | collective-permute-start | bytes 1419272 | tf_op jit(solution)/shard_map/ppermute | solution.py:207
  86.5 0.8 copy-start.5
  87.2 10.3 %collective-permute-start.9 = (bf16[264,896]{1,0:T(8,128)(2,1)}, bf16[264,896]{1,0:T(8,128)(2,1)}, u32[]{:S(2)}, u32[]{:S(2)}) collective-permute-start(bf16[264,896]{1,0:T(8,128)(2,1)} %collective-permute-done.8.refs_5_), channel_id=1, source_target_pairs={{0,2},{1,15},{2,4},{3,1},{4,6},{5,3},{6,8},{7,5},{8,10},{9,7},{10,... | collective-permute-start | bytes 1419272 | tf_op jit(solution)/shard_map/ppermute | solution.py:209
  92.0 13.2 %collective-permute-start.5 = (bf16[264,896]{1,0:T(8,128)(2,1)}, bf16[264,896]{1,0:T(8,128)(2,1)S(1)}, u32[]{:S(2)}, u32[]{:S(2)}) collective-permute-start(bf16[264,896]{1,0:T(8,128)(2,1)} %collective-permute-done.4.refs_3_), channel_id=1, source_target_pairs={{0,2},{1,15},{2,4},{3,1},{4,6},{5,3},{6,8},{7,5},{8,10},{9,7},{10,... | collective-permute-start | bytes 1419272 | tf_op jit(solution)/shard_map/ppermute | solution.py:207
  97.5 1.5 %copy-start = (bf16[128,7168]{1,0:T(8,128)(2,1)S(1)}, bf16[128,7168]{1,0:T(8,128)(2,1)}, u32[]{:S(2)}) copy-start(bf16[128,7168]{1,0:T(8,128)(2,1)} %own_w.1) | copy-start | bytes 5505028
  99.0 0.9 copy-start.2
  99.9 1.0 copy-start.4
  100.9 1.0 copy-start.6
  107.7 0.6 copy-start.7
  108.4 17.7 %all-to-all-start.1 = ((f32[16,1,128]{2,1,0:T(1,128)}), f32[16,1,128]{2,1,0:T(1,128)S(1)}, u32[]{:S(2)}, u32[]{:S(2)}) async-start(f32[16,1,128]{2,1,0:T(1,128)} %get-tuple-element.13), calls=%async_computation.1 | async-start | bytes 16384 | tf_op jit(solution)/shard_map/all_to_all | solution.py:235
  119.1 14.3 %collective-permute-start.10 = (bf16[256,128]{1,0:T(8,128)(2,1)S(1)}, bf16[256,128]{1,0:T(8,128)(2,1)S(1)}, u32[]{:S(2)}, u32[]{:S(2)}) collective-permute-start(bf16[256,128]{1,0:T(8,128)(2,1)S(1)} %get-tuple-element.12), channel_id=1, source_target_pairs={{0,1},{1,0},{2,3},{3,2},{4,5},{5,4},{6,7},{7,6},{8,9},{9,8},{10,11... | collective-permute-start | bytes 196616 | tf_op jit(solution)/shard_map/ppermute | solution.py:234
  126.8 17.0 %all-to-all-start.2 = ((f32[64,1,128]{2,1,0:T(1,128)}), f32[64,1,128]{2,1,0:T(1,128)S(1)}, u32[]{:S(2)}, u32[]{:S(2)}) async-start(f32[64,1,128]{2,1,0:T(1,128)} %broadcast_in_dim.12), calls=%async_computation.2 | async-start | bytes 65536 | tf_op jit(solution)/shard_map/all_to_all | solution.py:238
